TPU v7x, 128 devices: a whole 4x4x4 slice. The times are simulated.
128 devices in a mesh: blk: 64 (over x, y, z_lo, core), rep: 2 (over z_hi).
Axes of the slice: x: 4, y: 4, z: 4 (z_hi: 2, z_lo: 2; z = z_hi * 2 + z_lo), core: 2. Of those that a mesh axis runs over, the one named last changes fastest.
Arguments:
- points: bfloat16 [64, 49152], P(None, ('blk', 'rep')), may hold values from -6 to 6
- targets: float32 [32, 49152], P(None, ('blk', 'rep')), may hold values from -15 to 15
- cal_offset: int32 [16384], P(('blk', 'rep')), may hold values from 0 to 383
Outputs:
- coefficients: float32 [32, 49152], P(None, ('blk', 'rep'))
- residual: float32 [32, 49152], P(None, ('blk', 'rep'))
- scores: float32 [32, 16384], P(None, ('blk', 'rep'))
All inputs are finite; a program needn't handle non-finite values.
Results may differ from a plain program's by a relative error of at most 0.0008.
Values may be sent and summed in bfloat16 or wider, within the bound.
No kernel may reach another device: no remote copies, remote signals or barrier semaphores. Data moves between devices by JAX's collectives and lax.ppermute only.
A program may use at most 64 MiB of HBM per device.

v0:
```python
import functools

import jax
import jax.numpy as jnp
from jax import lax
from jax.experimental import pallas as pl
from jax.experimental.pallas import tpu as pltpu
from jax.sharding import Mesh, PartitionSpec as P

ALL = ("x", "y", "zl", "c", "zh")
Z = ("zl", "zh")
BF16, F32, F8 = jnp.bfloat16, jnp.float32, jnp.float8_e4m3fn
SHRINKAGE = 0.5
LOG2E = 1.4426950408889634
VM = pl.BlockSpec(memory_space=pltpu.VMEM)
HB = pl.BlockSpec(memory_space=pltpu.HBM)
TILE, ROWS, DEPTH = 512, 64, 4
NEAR, KEEP = (1, 1, 1, 5), 2
FORM_ROOM, APPLY_ROOM = 3 * 2**20, 1 * 2**20
SIDES, WIDTH, LANES = 32, 384, 128


def call(kernel, outs, limit, scratch=(), cost=None, in_specs=None, out_specs=None, name=None):
    if cost is not None:
        cost = pl.CostEstimate(flops=0, transcendentals=0, bytes_accessed=int(cost * 3.6e6))
    return lambda *args: pl.pallas_call(
        kernel,
        out_shape=outs,
        in_specs=in_specs or [VM] * len(args),
        out_specs=out_specs or [VM] * len(outs),
        scratch_shapes=scratch,
        compiler_params=pltpu.CompilerParams(vmem_limit_bytes=limit),
        cost_estimate=cost,
        name=name,
    )(*args)


def f32(*shape):
    return jax.ShapeDtypeStruct(shape, F32)


def swap(array, axis, k, size=4):
    return lax.ppermute(array, axis, [(i, i ^ k) for i in range(size)])


def round_of(array, axis):
    return [array] + [swap(array, axis, k) for k in (1, 3, 2)]


def split3(a):
    first = a.astype(BF16)
    rest = a - first.astype(F32)
    second = rest.astype(BF16)
    return first, second, (rest - second.astype(F32)).astype(BF16)


def tail_rows(first, second, n):
    rows = [part.astype(F32) for part in (*first, *second)]
    return jnp.concatenate([*rows, jnp.zeros((10, n), F32)], axis=0).astype(BF16)


def pack_kernel(points_ref, targets_ref, out_ref, targets, sems):
    copies = [
        pltpu.make_async_copy(points_ref, out_ref.at[0:64, :], sems.at[0]),
        pltpu.make_async_copy(targets_ref, targets, sems.at[1]),
    ]
    for copy in copies:
        copy.start()
    copies[1].wait()
    for place, part in enumerate(split3(targets[...])):
        out_ref[64 + place * SIDES : 64 + place * SIDES + SIDES, :] = part
    copies[0].wait()


def unpacked(ref):
    parts = [ref[64 + place * SIDES : 64 + place * SIDES + SIDES, :].astype(F32) for place in range(3)]
    return (parts[0] + parts[1]) + parts[2]


def prepare_kernel(sharpness, xi_ref, right):
    columns = xi_ref.shape[1]
    xi = xi_ref[...].astype(F32)
    sq = jnp.sum(xi * xi, axis=0, keepdims=True) * (-sharpness * LOG2E)
    for place, part in enumerate(split3(xi * (2.0 * sharpness * LOG2E))):
        right[place * 64 : place * 64 + 64, :] = part
    ones = [jnp.ones((1, columns), F32)] * 3
    right[192:208, :] = tail_rows(split3(sq), ones, columns)
    right[208:256, :] = jnp.zeros((48, columns), BF16)


def form_kernel(sharpness, kind, near, *refs):
    pack_ref, right, *refs = refs
    acc_ref, refs = (None, refs) if kind == "first" else (refs[0], refs[1:])
    tiles = right.shape[1] // TILE
    hi_refs, refs = refs[:tiles], refs[tiles:]
    near_refs, refs = refs[:near], refs[near:]
    far_ref, refs = (refs[0], refs[1:]) if near < tiles else (None, refs)
    out_ref, left_t, left, *own = refs
    if far_ref is not None:
        stage, sems = own
    count = pack_ref.shape[1]
    xj = pack_ref[0:64, :]
    xf = xj.astype(F32)
    sq = jnp.sum(xf * xf, axis=0, keepdims=True) * (-sharpness * LOG2E)
    for place in range(3):
        left_t[place * 64 : place * 64 + 64, :] = xj
    ones = [jnp.ones((1, count), F32)] * 3
    left_t[192:208, :] = tail_rows(ones, split3(sq), count)
    left_t[208:256, :] = jnp.zeros((48, count), BF16)
    for r in range(count // 128):
        at = slice(r * 128, r * 128 + 128)
        left[at, :] = left_t[:, at].T
    finish_tile(kind, sums_first, unpacked(pack_ref), (), acc_ref, None, out_ref)

    def copy(c, slot):
        return pltpu.make_async_copy(stage.at[slot], far_ref.at[c - near], sems.at[slot])

    def step(units, c, slot):
        starts = [pl.multiple_of(c * TILE + m * 256, 256) for m in range(2)]
        lows = near_refs[c] if slot is None else stage.at[slot]

        def finish(at, m, value):
            value = jnp.exp2(value)
            high = value.astype(BF16)
            hi_refs[c][at, m * 256 : m * 256 + 256] = high
            lows[at, m * 256 : m * 256 + 256] = (value - high.astype(F32)).astype(BF16)

        for m in range(2):
            pltpu.matmul_push_rhs(right[:, pl.ds(starts[m], 256)], 0, m)
        waiting = []
        for r in range(count // ROWS):
            at = slice(r * ROWS, r * ROWS + ROWS)
            for m in range(2):
                unit = units[m][r % DEPTH]
                pltpu.matmul_acc_lhs(unit, left[at, :], load_staged_rhs=0 if r == 0 else None)
                waiting.append((at, m, unit))
            if len(waiting) > 2 * (DEPTH - 1):
                for _ in range(2):
                    at, m, unit = waiting.pop(0)
                    finish(at, m, pltpu.matmul_pop(unit))
        for at, m, unit in waiting:
            finish(at, m, pltpu.matmul_pop(unit))
        turn = 0
        for k in range(count // 256):
            rows = slice(k * 256, k * 256 + 256)
            for source, which, height in ((hi_refs[c], -2, 96), (lows, -1, 64)):
                for m in range(2):
                    pltpu.matmul_push_rhs(source[rows, m * 256 : m * 256 + 256], turn % 2, m)
                for m in range(2):
                    pltpu.matmul_acc_lhs(units[m][which], pack_ref[64 : 64 + height, rows], load_staged_rhs=turn % 2)
                turn += 1
        for m in range(2):
            a, b = pltpu.matmul_pop(units[m][-2]), pltpu.matmul_pop(units[m][-1])
            value = a[0:SIDES] + (a[SIDES : 2 * SIDES] + ((b[0:SIDES] + b[SIDES:]) + a[2 * SIDES :]))
            if acc_ref is not None:
                value = value + acc_ref[:, pl.ds(starts[m], 256)]
            out_ref[:, pl.ds(starts[m], 256)] = value

    def steps(*units):
        each = len(units) // 2
        units = (units[:each], units[each:])
        for c in range(near, tiles):
            slot = (c - near) % KEEP
            if c >= near + KEEP:
                copy(c - KEEP, slot).wait()
            step(units, c, slot)
            copy(c, slot).start()
        for c in range(near):
            step(units, c, None)
        for c in range(max(near, tiles - KEEP), tiles):
            copy(c, (c - near) % KEEP).wait()

    heights = [ROWS] * DEPTH + [96, 64]
    pl.run_scoped(steps, *[pltpu.ACC(m)((h, 256), F32) for m in range(2) for h in heights])


def finish_tile(kind, sums, v, extra, acc_ref, tile_ref, out_ref):
    width = out_ref.shape[1] - LANES
    if kind == "own":
        tile = tile_ref[:, tile_ref.shape[1] - LANES :]
    else:
        tile = in_lanes(*sums(v, *extra))
        if acc_ref is not None:
            tile = tile + acc_ref[:, acc_ref.shape[1] - LANES :]
    out_ref[:, width:] = tile


def form(kind, near, pack, right, acc):
    count, width = pack.shape[1], right.shape[1]
    tiles = width // TILE
    outs = [pltpu.VMEM((count, TILE), BF16)] * (tiles + near)
    specs = [VM] * (tiles + near)
    scratch = [pltpu.VMEM((256, count), BF16), pltpu.VMEM((count, 256), BF16)]
    keep = min(KEEP, tiles - near)
    if keep:
        outs.append(pltpu.HBM((tiles - near, count, TILE), BF16))
        specs.append(HB)
        scratch += [pltpu.VMEM((keep, count, TILE), BF16), pltpu.SemaphoreType.DMA((keep,))]
    *parts, out = call(
        functools.partial(form_kernel, 3.0 / 64, kind, near),
        outs + [f32(SIDES, width + LANES)],
        FORM_ROOM + 3 * 2**19 * keep,
        scratch,
        cost=8.5,
        out_specs=specs + [VM],
        name="form",
    )(pack, right, *acc)
    return (parts[:tiles], parts[tiles : tiles + near], parts[tiles + near :]), out


def apply_kernel(sums, kind, columns, n_extra, all_tiles, near, *refs):
    v_ref, *refs = refs
    extra, refs = refs[:n_extra], refs[n_extra:]
    hi_refs, refs = refs[:all_tiles], refs[all_tiles:]
    near_refs, refs = refs[:near], refs[near:]
    far_ref, refs = (refs[0], refs[1:]) if near < all_tiles else (None, refs)
    acc_ref, refs = (None, refs) if kind == "first" else (refs[0], refs[1:])
    tile_ref, refs = (refs[0], refs[1:]) if kind == "own" else (None, refs)
    out_ref, parts, *own = refs
    if own:
        slots, sems = own
    tiles = range(columns // TILE, (columns + out_ref.shape[1] - LANES) // TILE)
    far_tiles = [c for c in tiles if c >= near]

    def copy(c):
        slot = c - far_tiles[0]
        return pltpu.make_async_copy(far_ref.at[c - near], slots.at[slot], sems.at[slot])

    for c in far_tiles:
        copy(c).start()
    v = v_ref[...]
    for place, part in enumerate(split3(v)):
        parts[place * SIDES : place * SIDES + SIDES, :] = part
    for c in tiles:
        cols, from_cols = (slice(at, at + TILE) for at in (c * TILE - columns, c * TILE))
        a = jnp.dot(parts[...], hi_refs[c][...], preferred_element_type=F32)
        value = a[0:SIDES] + (a[SIDES : 2 * SIDES] + a[2 * SIDES :])
        if acc_ref is not None:
            value = value + acc_ref[:, from_cols]
        out_ref[:, cols] = value
    finish_tile(kind, sums, v, extra, acc_ref, tile_ref, out_ref)
    for c in tiles:
        cols, from_cols = (slice(at, at + TILE) for at in (c * TILE - columns, c * TILE))
        if c >= near:
            copy(c).wait()
            low = slots[c - far_tiles[0]]
        else:
            low = near_refs[c][...]
        b = jnp.dot(parts[0 : 2 * SIDES, :], low, preferred_element_type=F32)
        out_ref[:, cols] = out_ref[:, cols] + (b[0:SIDES] + b[SIDES:])


def apply_block(sums, kind, columns, width, v, extra, hi, near, far, acc, tile):
    count = hi[0].shape[0]
    slots = sum(c >= len(near) for c in range(columns // TILE, (columns + width) // TILE))
    scratch = [pltpu.VMEM((3 * SIDES, count), BF16)]
    if slots:
        scratch += [pltpu.VMEM((slots, count, TILE), BF16), pltpu.SemaphoreType.DMA((slots,))]
    args, specs = [v, *extra, *hi], [VM] * (1 + len(extra) + len(hi))
    args += [*near, *[pltpu.with_memory_space_constraint(array, pltpu.HBM) for array in far]]
    specs += [VM] * len(near) + [HB] * len(far)
    return call(
        functools.partial(apply_kernel, sums, kind, columns, len(extra), len(hi), len(near)),
        [f32(SIDES, width + LANES)],
        APPLY_ROOM + 3 * 2**19 * slots,
        scratch,
        cost=(4.4 if slots else 3.2) * width / 3072,
        in_specs=specs + [VM] * len(acc + tile),
        name="apply",
    )(*args, *acc, *tile)[0]


def summed(own, other):
    fold = call(fold_kernel, [f32(SIDES, WIDTH + LANES)] * 4, 2**20, name="fold")
    parts = fold(own, swap(other, "c", 1, 2))
    return [parts[0]] + [swap(parts[m], Z, m) for m in (1, 3, 2)]


def first_product(packs, right):
    blocks, acc = [], []
    for k, pack in enumerate(packs):
        block, out = form("next" if k else "first", NEAR[k], pack, right, acc)
        blocks.append(block)
        acc = [out]
    half = 4 * WIDTH
    halves = [jnp.concatenate([out[:, at : at + half], out[:, 2 * half :]], axis=1) for at in (0, half)]
    return summed(*halves), blocks


def product(sums, vectors, extras, blocks, common=()):
    half, last = 4 * WIDTH, len(vectors) - 1

    def work(kind, k, columns, width, acc, tile):
        extra = [e[k] for e in extras] + list(common)
        return apply_block(sums, kind, columns, width, vectors[k], extra, *blocks[k], acc, tile)

    acc = []
    for k in range(last):
        acc = [work("next" if k else "first", k, 0, 2 * half, acc, [])]
    other = work("other", last, half, half, acc, [])
    return summed(work("own", last, 0, half, acc, [other]), other)


def fold_kernel(own_ref, got_ref, *outs):
    value = own_ref[...] + got_ref[...]
    for m, out in enumerate(outs):
        out[:, :WIDTH] = value[:, m * WIDTH : m * WIDTH + WIDTH]
        out[:, WIDTH:] = value[:, 4 * WIDTH :]


def total(a):
    return jnp.sum(a, axis=1, keepdims=True)


def in_lanes(*values):
    lane = lax.broadcasted_iota(jnp.int32, (SIDES, LANES), 1)
    tile = jnp.zeros((SIDES, LANES), F32)
    for place, value in enumerate(values):
        tile = jnp.where(lane == place, value, tile)
    return tile


def sums_first(v):
    return (total(v * v),)


def sums_second(v, b_ref):
    return total(unpacked(b_ref) * v), total(v * v)


def sums_third(v, b_ref, u0_ref, coef):
    b, u0 = unpacked(b_ref), u0_ref[...]
    r1 = b - coef[:, 0:1] * u0
    d1 = r1 + coef[:, 1:2] * b
    return total(d1 * v), total(v * v), total(r1 * v), total(r1 * r1)


def gather_plane(array):
    return round_of(jnp.concatenate(round_of(array, "y"), axis=1), "x")


def added(refs):
    got = (refs[0][...] + refs[1][...]) + (refs[2][...] + refs[3][...])
    return got[:, :WIDTH], got[:, WIDTH:]


def first_kernel(m0, m1, m2, m3, b_ref, u_ref, sums_ref):
    got, sums_ref[...] = added((m0, m1, m2, m3))
    u_ref[...] = got + SHRINKAGE * b_ref[...]


def second_kernel(m0, m1, m2, m3, b_ref, u0_ref, sums_ref, u1_ref, r1_ref, d1_ref, ar1_ref, coef_ref):
    got, sums = added((m0, m1, m2, m3))
    b, u0 = b_ref[...], u0_ref[...]
    y = got + SHRINKAGE * u0
    rr0, c0, q0 = sums_ref[:, 0:1], sums[:, 0:1], sums[:, 1:2]
    a0 = rr0 / c0
    rr1 = rr0 - 2.0 * a0 * c0 + a0 * a0 * q0
    b0 = rr1 / rr0
    r1 = b - a0 * u0
    ar1 = u0 - a0 * y
    r1_ref[...] = r1
    d1_ref[...] = r1 + b0 * b
    ar1_ref[...] = ar1
    u1_ref[...] = ar1 + b0 * u0
    coef_ref[...] = in_lanes(a0, b0)


def third_kernel(
    m0, m1, m2, m3, b_ref, u1_ref, r1_ref, d1_ref, ar1_ref, coef_ref, x2_ref, r2_ref, d2_ref, u2_ref, sums_ref
):
    got, sums = added((m0, m1, m2, m3))
    u1, d1, r1 = u1_ref[...], d1_ref[...], r1_ref[...]
    y = got + SHRINKAGE * u1
    c1, q1, p1, rr1 = (sums[:, k : k + 1] for k in range(4))
    a1 = rr1 / c1
    rr2 = rr1 - 2.0 * a1 * p1 + a1 * a1 * q1
    b1 = rr2 / rr1
    r2 = r1 - a1 * u1
    d2 = r2 + b1 * d1
    u2 = (ar1_ref[...] - a1 * y) + b1 * u1
    x2_ref[...] = coef_ref[:, 0:1] * b_ref[...] + a1 * d1
    r2_ref[...] = r2
    d2_ref[...] = d2
    u2_ref[...] = u2
    tile = jnp.concatenate([in_lanes(total(d2 * u2), total(r2 * r2)), jnp.zeros((LANES - SIDES, LANES), F32)], axis=0)
    sums_ref[...] = jnp.transpose(tile)[0:8, :]


def last_kernel(sums_ref, x2_ref, r2_ref, d2_ref, u2_ref, at_ref, x_ref, r_ref, s_ref):
    got = jnp.transpose(jnp.sum(sums_ref[...], axis=0))[0:SIDES, :]
    a2 = got[:, 1:2] / got[:, 0:1]
    x = x2_ref[...] + a2 * d2_ref[...]
    r = r2_ref[...] - a2 * u2_ref[...]
    x_ref[...] = x
    r_ref[...] = r
    place = lax.broadcasted_iota(jnp.int32, (WIDTH, LANES), 0)
    pick = jnp.where(place == at_ref[...], 1.0, 0.0).astype(BF16)
    parts = [jnp.dot(p, pick, preferred_element_type=F32) for p in split3(r + SHRINKAGE * x)]
    s_ref[...] = jnp.abs((parts[0] + parts[1]) + parts[2])


def body(points, targets, cal_offset):
    small = 4 * 2**20
    vector = f32(SIDES, WIDTH)
    tile = f32(SIDES, LANES)
    b = targets
    scratch = [pltpu.VMEM((SIDES, WIDTH), F32), pltpu.SemaphoreType.DMA((2,))]
    outs = [jax.ShapeDtypeStruct((160, WIDTH), BF16)]
    in_hbm = [pltpu.with_memory_space_constraint(array, pltpu.HBM) for array in (points, b)]
    pack = call(pack_kernel, outs, small, scratch, in_specs=[HB, HB], name="pack")(*in_hbm)[0]
    bj = gather_plane(pack)
    pair = jnp.concatenate([pack[0:64], swap(points, "c", 1, 2)], axis=1)
    pairs = [pair] + [swap(pair, Z, m) for m in (1, 2, 3)]
    xi = jnp.concatenate([p[:, :WIDTH] for p in pairs] + [p[:, WIDTH:] for p in pairs], axis=1)
    prepare = functools.partial(prepare_kernel, 3.0 / points.shape[0])
    right = call(prepare, [jax.ShapeDtypeStruct((256, xi.shape[1]), BF16)], small, name="prepare")(xi)[0]
    msgs, blocks = first_product(bj, right)
    u0, sums = call(first_kernel, [vector, tile], small, name="first")(*msgs, b)
    u0j = gather_plane(u0)
    msgs = product(sums_second, u0j, [bj], blocks)
    u1, r1, d1, ar1, coef = call(second_kernel, [vector] * 4 + [tile], small, name="second")(*msgs, b, u0, sums)
    msgs = product(sums_third, gather_plane(u1), [bj, u0j], blocks, (coef,))
    x2, r2, d2, u2, part = call(third_kernel, [vector] * 4 + [f32(8, LANES)], small, name="third")(
        *msgs, b, u1, r1, d1, ar1, coef
    )
    part = part + swap(part, "c", 1, 2)
    parts = lax.all_to_all(
        jnp.broadcast_to(part[None], (64, 8, LANES)), ("x", "y", *Z), split_axis=0, concat_axis=0, tiled=True
    )
    return tuple(
        call(last_kernel, [vector, vector, tile], small, name="last")(
            parts, x2, r2, d2, u2, cal_offset.reshape(1, LANES)
        )
    )


def solution(mesh):
    grid = Mesh(mesh.devices.reshape(4, 4, 2, 2, 2), ALL)
    return jax.shard_map(
        body,
        mesh=grid,
        in_specs=(P(None, ALL), P(None, ALL), P(ALL)),
        out_specs=(P(None, ALL), P(None, ALL), P(None, ALL)),
        check_vma=False,
    )
```

profile of v0, /device:TPU:0, one launch (start us, length us, event | category | flops | bytes accessed | tf_op | source)
XLA Modules:
  0.0 162.8 jit_solution(17496001348824460994)
XLA Ops:
  1.6 3.4 %collective-permute-start.2 = (bf16[160,384]{1,0:T(8,128)(2,1)S(1)}, bf16[160,384]{1,0:T(8,128)(2,1)S(1)}, u32[]{:S(2)}, u32[]{:S(2)}) collective-permute-start(bf16[160,384]{1,0:T(8,128)(2,1)S(1)} %pack.1), channel_id=1, source_target_pairs={{0,16},{8,24},{16,0},{24,8},{1,17},{9,25},{17,1},{25,9},{2,18},{10... | collective-permute-start | bytes 368648 | tf_op jit(solution)/shard_map/ppermute | solution.py:43
  6.0 4.1 %collective-permute-start.7 = (bf16[64,768]{1,0:T(8,128)(2,1)S(1)}, bf16[64,768]{1,0:T(8,128)(2,1)S(1)}, u32[]{:S(2)}, u32[]{:S(2)}) collective-permute-start(bf16[64,768]{1,0:T(8,128)(2,1)S(1)} %pad_maximum_fusion.2), channel_id=1, source_target_pairs={{0,5},{1,4},{4,1},{5,0},{2,7},{3,6},{6,3},{7,2},{8,13},{9,12},{12,... | collective-permute-start | bytes 294920 | tf_op jit(solution)/shard_map/ppermute | solution.py:43
  10.2 2.7 %collective-permute-start.5 = (bf16[64,768]{1,0:T(8,128)(2,1)S(1)}, bf16[64,768]{1,0:T(8,128)(2,1)S(1)}, u32[]{:S(2)}, u32[]{:S(2)}) collective-permute-start(bf16[64,768]{1,0:T(8,128)(2,1)S(1)} %pad_maximum_fusion.2), channel_id=1, source_target_pairs={{0,1},{1,0},{4,5},{5,4},{2,3},{3,2},{6,7},{7,6},{8,9},{9,8},{12,13... | collective-permute-start | bytes 294920 | tf_op jit(solution)/shard_map/ppermute | solution.py:43
  16.6 3.0 %collective-permute-start.3 = (bf16[160,1536]{1,0:T(8,128)(2,1)S(1)}, bf16[160,1536]{1,0:T(8,128)(2,1)S(1)}, u32[]{:S(2)}, u32[]{:S(2)}) collective-permute-start(bf16[160,1536]{1,0:T(8,128)(2,1)S(1)} %pad_maximum_fusion.refs_0_.refs_1_), channel_id=1, source_target_pairs={{0,64},{32,96},{64,0},{96,32},{1,65},{33,97},{65,1},{97,33},{2,66}... | collective-permute-start | bytes 1474568 | tf_op jit(solution)/shard_map/ppermute | solution.py:43
  20.1 7.6 %form.4 = (bf16[1536,512]{1,0:T(8,128)(2,1)S(1)}, bf16[1536,512]{1,0:T(8,128)(2,1)S(1)}, bf16[1536,512]{1,0:T(8,128)(2,1)S(1)}, bf16[1536,512]{1,0:T(8,128)(2,1)...) custom-call(bf16[160,1536]{1,0:T(8,128)(2,1)S(1)} %pad_maximum_fusio, ...), custom_call_target="tpu_custom_call" | custom-call | bytes 30600000 | tf_op jit(solution)/shard_map/form/pallas_call | solution.py:26
  28.9 8.0 %form.5 = (bf16[1536,512]{1,0:T(8,128)(2,1)S(1)}, bf16[1536,512]{1,0:T(8,128)(2,1)S(1)}, bf16[1536,512]{1,0:T(8,128)(2,1)S(1)}, bf16[1536,512]{1,0:T(8,128)(2,1)...) custom-call(bf16[160,1536]{1,0:T(8,128)(2,1)S(1)} %collective-permut, ...), custom_call_target="tpu_custom_call" | custom-call | bytes 30600000 | tf_op jit(solution)/shard_map/form/pallas_call | solution.py:26
  38.5 7.6 %form.6 = (bf16[1536,512]{1,0:T(8,128)(2,1)S(1)}, bf16[1536,512]{1,0:T(8,128)(2,1)S(1)}, bf16[1536,512]{1,0:T(8,128)(2,1)S(1)}, bf16[1536,512]{1,0:T(8,128)(2,1)...) custom-call(bf16[160,1536]{1,0:T(8,128)(2,1)S(1)} %collective-permut, ...), custom_call_target="tpu_custom_call" | custom-call | bytes 30600000 | tf_op jit(solution)/shard_map/form/pallas_call | solution.py:26
  46.2 7.2 %form.7 = (bf16[1536,512]{1,0:T(8,128)(2,1)S(1)}, bf16[1536,512]{1,0:T(8,128)(2,1)S(1)}, bf16[1536,512]{1,0:T(8,128)(2,1)S(1)}, bf16[1536,512]{1,0:T(8,128)(2,1)...) custom-call(bf16[160,1536]{1,0:T(8,128)(2,1)S(1)} %collective-permut, ...), custom_call_target="tpu_custom_call" | custom-call | bytes 30600000 | tf_op jit(solution)/shard_map/form/pallas_call | solution.py:26
  55.1 3.3 %collective-permute-start.11 = (f32[32,512]{1,0:T(8,128)S(1)}, f32[32,512]{1,0:T(8,128)S(1)}, u32[]{:S(2)}, u32[]{:S(2)}) collective-permute-start(f32[32,512]{1,0:T(8,128)S(1)} %get-tuple-element.72), channel_id=1, source_target_pairs={{0,1},{1,0},{4,5},{5,4},{2,3},{3,2},{6,7},{7,6},{8,9},{9,8},{12,13... | collective-permute-start | bytes 196616 | tf_op jit(solution)/shard_map/ppermute | solution.py:43
  61.0 3.0 %collective-permute-done.12.m2 = f32[32,512]{1,0:T(8,128)S(1)} collective-permute-done((f32[32,512]{1,0:T(8,128)S(1)}, f32[32,512]{1,0:T(8,128)S(1)}, u32[]{:S(2)}, u32[]{:S(2)}) %collective-permute-start.12) | collective-permute-done | bytes 65568 | tf_op jit(solution)/shard_map/ppermute | solution.py:43
  64.0 2.5 %collective-permute-start.16 = (f32[32,384]{1,0:T(8,128)S(1)}, f32[32,384]{1,0:T(8,128)S(1)}, u32[]{:S(2)}, u32[]{:S(2)}) collective-permute-start(f32[32,384]{1,0:T(8,128)S(1)} %get-tuple-element.75.u0_ref), channel_id=1, source_target_pairs={{0,16},{8,24},{16,0},{24,8},{1,17},{9,25},{17,1},{25,9},{2,18},{10... | collective-permute-start | bytes 147464 | tf_op jit(solution)/shard_map/ppermute | solution.py:43
  68.3 4.1 %collective-permute-done.14 = f32[32,384]{1,0:T(8,128)S(1)} collective-permute-done((f32[32,384]{1,0:T(8,128)S(1)}, f32[32,384]{1,0:T(8,128)S(1)}, u32[]{:S(2)}, u32[]{:S(2)}) %collective-permute-start.14) | collective-permute-done | bytes 49184 | tf_op jit(solution)/shard_map/ppermute | solution.py:43
  72.5 2.2 %collective-permute-start.18 = (f32[32,1536]{1,0:T(8,128)S(1)}, f32[32,1536]{1,0:T(8,128)S(1)}, u32[]{:S(2)}, u32[]{:S(2)}) collective-permute-start(f32[32,1536]{1,0:T(8,128)S(1)} %constant_dynamic-update-slice_fusion.2.refs_0_.refs_2_), channel_id=1, source_target_pairs={{0,96},{32,64},{64,32},{96,0},{1,97},{33,65},{65,33},{97,1},{2,98}... | collective-permute-start | bytes 589832 | tf_op jit(solution)/shard_map/ppermute | solution.py:43
  76.6 4.3 %apply.10.refs_10_ = f32[32,3200]{1,0:T(8,128)S(1)} custom-call(f32[32,1536]{1,0:T(8,128)S(1)} %constant_dynamic-update-slice_fusion.2.refs_0_.refs_2_, bf16[160,1536]{1,0:T(8,128)(2,1)S(1)} %pad_maximum_fusion.refs_0_.refs_1_, bf16[1536,512]{1,0:T(8,128)(2,1)S(1)} %get-tuple-element.104.refs_2_.refs_4_, bf16[1536,512]{1,0:T(8,128)(2,1)S(1)} %copy-done.1, ...), custom_call_target="tpu_custom_call" | custom-call | bytes 15840000 | tf_op jit(solution)/shard_map/apply/pallas_call | solution.py:26
  81.0 4.6 %apply.11.refs_10_ = f32[32,3200]{1,0:T(8,128)S(1)} custom-call(f32[32,1536]{1,0:T(8,128)S(1)} %collective-permute-done.19.refs_0_.refs_2_, bf16[160,1536]{1,0:T(8,128)(2,1)S(1)} %collective-permute-done.9.refs_0_.refs_1_, bf16[1536,512]{1,0:T(8,128)(2,1)S(1)} %get-tuple-element.96.refs_2_.refs_4_, bf16[1536,512]{1,0:T(8,128)(2,1)S(1)} %get-tuple-element.97.refs_3_.refs_5_, ...), custom_call_target="tpu_custom_call" | custom-call | bytes 15840000 | tf_op jit(solution)/shard_map/apply/pallas_call | solution.py:26
  85.6 4.6 %apply.12.refs_14_ = f32[32,3200]{1,0:T(8,128)S(1)} custom-call(f32[32,1536]{1,0:T(8,128)S(1)} %collective-permute-done.18.refs_0_.refs_2_, bf16[160,1536]{1,0:T(8,128)(2,1)S(1)} %collective-permute-done.8.refs_0_.refs_1_, bf16[1536,512]{1,0:T(8,128)(2,1)S(1)} %get-tuple-element.88.refs_2_.refs_4_, bf16[1536,512]{1,0:T(8,128)(2,1)S(1)} %get-tuple-element.89.refs_3_.refs_5_, ...), custom_call_target="tpu_custom_call" | custom-call | bytes 15840000 | tf_op jit(solution)/shard_map/apply/pallas_call | solution.py:26
  97.4 2.5 %collective-permute-done.21.m1 = f32[32,512]{1,0:T(8,128)S(1)} collective-permute-done((f32[32,512]{1,0:T(8,128)S(1)}, f32[32,512]{1,0:T(8,128)S(1)}, u32[]{:S(2)}, u32[]{:S(2)}) %collective-permute-start.21) | collective-permute-done | bytes 65568 | tf_op jit(solution)/shard_map/ppermute | solution.py:43
  105.2 3.3 %collective-permute-done.24 = f32[32,384]{1,0:T(8,128)S(1)} collective-permute-done((f32[32,384]{1,0:T(8,128)S(1)}, f32[32,384]{1,0:T(8,128)S(1)}, u32[]{:S(2)}, u32[]{:S(2)}) %collective-permute-start.24) | collective-permute-done | bytes 49184 | tf_op jit(solution)/shard_map/ppermute | solution.py:43
  114.3 5.5 %apply.15.refs_12_ = f32[32,3200]{1,0:T(8,128)S(1)} custom-call(f32[32,1536]{1,0:T(8,128)S(1)} %constant_dynamic-update-slice_fusion.6.refs_0_, bf16[160,1536]{1,0:T(8,128)(2,1)S(1)} %pad_maximum_fusion.refs_0_.refs_1_, f32[32,1536]{1,0:T(8,128)S(1)} %constant_dynamic-update-slice_fusion.2.refs_0_.refs_2_, ...), custom_call_target="tpu_custom_call" | custom-call | bytes 15840000 | tf_op jit(solution)/shard_map/apply/pallas_call | solution.py:26
  119.8 4.8 %apply.16.refs_12_ = f32[32,3200]{1,0:T(8,128)S(1)} custom-call(f32[32,1536]{1,0:T(8,128)S(1)} %collective-permute-done.29.refs_0_, bf16[160,1536]{1,0:T(8,128)(2,1)S(1)} %collective-permute-done.9.refs_0_.refs_1_, f32[32,1536]{1,0:T(8,128)S(1)} %collective-permute-done.19.refs_0_.refs_2_, f32[32,128]{1,0:T(8,128)S(1)} %get-tuple-element.118.refs_3_.coef_ref, ...), custom_call_target="tpu_custom_call" | custom-call | bytes 15840000 | tf_op jit(solution)/shard_map/apply/pallas_call | solution.py:26
  124.7 4.8 %apply.17.refs_16_ = f32[32,3200]{1,0:T(8,128)S(1)} custom-call(f32[32,1536]{1,0:T(8,128)S(1)} %collective-permute-done.28.refs_0_, bf16[160,1536]{1,0:T(8,128)(2,1)S(1)} %collective-permute-done.8.refs_0_.refs_1_, f32[32,1536]{1,0:T(8,128)S(1)} %collective-permute-done.18.refs_0_.refs_2_, f32[32,128]{1,0:T(8,128)S(1)} %get-tuple-element.118.refs_3_.coef_ref, ...), custom_call_target="tpu_custom_call" | custom-call | bytes 15840000 | tf_op jit(solution)/shard_map/apply/pallas_call | solution.py:26
  129.5 3.1 %apply.18.refs_17_ = f32[32,1664]{1,0:T(8,128)S(1)} custom-call(f32[32,1536]{1,0:T(8,128)S(1)} %collective-permute-done.27.refs_0_, bf16[160,1536]{1,0:T(8,128)(2,1)S(1)} %collective-permute-done.3.refs_0_.refs_1_, f32[32,1536]{1,0:T(8,128)S(1)} %collective-permute-done.17.refs_0_.refs_2_, f32[32,128]{1,0:T(8,128)S(1)} %get-tuple-element.118.refs_3_.coef_ref, ...), custom_call_target="tpu_custom_call" | custom-call | bytes 7920000 | tf_op jit(solution)/shard_map/apply/pallas_call | solution.py:26
  138.1 2.5 %collective-permute-done.31.m1 = f32[32,512]{1,0:T(8,128)S(1)} collective-permute-done((f32[32,512]{1,0:T(8,128)S(1)}, f32[32,512]{1,0:T(8,128)S(1)}, u32[]{:S(2)}, u32[]{:S(2)}) %collective-permute-start.31) | collective-permute-done | bytes 65568 | tf_op jit(solution)/shard_map/ppermute | solution.py:43
  143.5 18.0 %all_to_all.5.sums_ref = f32[64,8,128]{2,1,0:T(8,128)S(1)} all-to-all(f32[64,8,128]{2,1,0:T(8,128)S(1)} %broadcast_in_dim.2), channel_id=1, replica_groups=mesh['x'=4,'y'=4,'zl'=2,'c'=2,'zh'=2] {'x','y','zl','zh'}, dimensions={0} | all-to-all | bytes 524288 | tf_op jit(solution)/shard_map/all_to_all | solution.py:428
  (106 shorter events, 44.6 us)
Async XLA Ops:
  1.6 8.6 %collective-permute-start.2 = (bf16[160,384]{1,0:T(8,128)(2,1)S(1)}, bf16[160,384]{1,0:T(8,128)(2,1)S(1)}, u32[]{:S(2)}, u32[]{:S(2)}) collective-permute-start(bf16[160,384]{1,0:T(8,128)(2,1)S(1)} %pack.1), channel_id=1, source_target_pairs={{0,16},{8,24},{16,0},{24,8},{1,17},{9,25},{17,1},{25,9},{2,18},{10... | collective-permute-start | bytes 368648 | tf_op jit(solution)/shard_map/ppermute | solution.py:43
  4.9 7.9 %collective-permute-start.1 = (bf16[160,384]{1,0:T(8,128)(2,1)S(1)}, bf16[160,384]{1,0:T(8,128)(2,1)S(1)}, u32[]{:S(2)}, u32[]{:S(2)}) collective-permute-start(bf16[160,384]{1,0:T(8,128)(2,1)S(1)} %pack.1), channel_id=1, source_target_pairs={{0,24},{8,16},{16,8},{24,0},{1,25},{9,17},{17,9},{25,1},{2,26},{10... | collective-permute-start | bytes 368648 | tf_op jit(solution)/shard_map/ppermute | solution.py:43
  6.0 6.9 %collective-permute-start = (bf16[160,384]{1,0:T(8,128)(2,1)S(1)}, bf16[160,384]{1,0:T(8,128)(2,1)S(1)}, u32[]{:S(2)}, u32[]{:S(2)}) collective-permute-start(bf16[160,384]{1,0:T(8,128)(2,1)S(1)} %pack.1), channel_id=1, source_target_pairs={{0,8},{8,0},{16,24},{24,16},{1,9},{9,1},{17,25},{25,17},{2,10},{10... | collective-permute-start | bytes 368648 | tf_op jit(solution)/shard_map/ppermute | solution.py:43
  6.0 13.6 %collective-permute-start.7 = (bf16[64,768]{1,0:T(8,128)(2,1)S(1)}, bf16[64,768]{1,0:T(8,128)(2,1)S(1)}, u32[]{:S(2)}, u32[]{:S(2)}) collective-permute-start(bf16[64,768]{1,0:T(8,128)(2,1)S(1)} %pad_maximum_fusion.2), channel_id=1, source_target_pairs={{0,5},{1,4},{4,1},{5,0},{2,7},{3,6},{6,3},{7,2},{8,13},{9,12},{12,... | collective-permute-start | bytes 294920 | tf_op jit(solution)/shard_map/ppermute | solution.py:43
  10.2 9.5 %collective-permute-start.6 = (bf16[64,768]{1,0:T(8,128)(2,1)S(1)}, bf16[64,768]{1,0:T(8,128)(2,1)S(1)}, u32[]{:S(2)}, u32[]{:S(2)}) collective-permute-start(bf16[64,768]{1,0:T(8,128)(2,1)S(1)} %pad_maximum_fusion.2), channel_id=1, source_target_pairs={{0,4},{1,5},{4,0},{5,1},{2,6},{3,7},{6,2},{7,3},{8,12},{9,13},{12,... | collective-permute-start | bytes 294920 | tf_op jit(solution)/shard_map/ppermute | solution.py:43
  10.2 6.4 %collective-permute-start.5 = (bf16[64,768]{1,0:T(8,128)(2,1)S(1)}, bf16[64,768]{1,0:T(8,128)(2,1)S(1)}, u32[]{:S(2)}, u32[]{:S(2)}) collective-permute-start(bf16[64,768]{1,0:T(8,128)(2,1)S(1)} %pad_maximum_fusion.2), channel_id=1, source_target_pairs={{0,1},{1,0},{4,5},{5,4},{2,3},{3,2},{6,7},{7,6},{8,9},{9,8},{12,13... | collective-permute-start | bytes 294920 | tf_op jit(solution)/shard_map/ppermute | solution.py:43
  12.9 16.0 %collective-permute-start.9 = (bf16[160,1536]{1,0:T(8,128)(2,1)S(1)}, bf16[160,1536]{1,0:T(8,128)(2,1)S(1)}, u32[]{:S(2)}, u32[]{:S(2)}) collective-permute-start(bf16[160,1536]{1,0:T(8,128)(2,1)S(1)} %pad_maximum_fusion.refs_0_.refs_1_), channel_id=1, source_target_pairs={{0,32},{32,0},{64,96},{96,64},{1,33},{33,1},{65,97},{97,65},{2,34}... | collective-permute-start | bytes 1474568 | tf_op jit(solution)/shard_map/ppermute | solution.py:43
  14.5 24.0 %collective-permute-start.8 = (bf16[160,1536]{1,0:T(8,128)(2,1)S(1)}, bf16[160,1536]{1,0:T(8,128)(2,1)S(1)}, u32[]{:S(2)}, u32[]{:S(2)}) collective-permute-start(bf16[160,1536]{1,0:T(8,128)(2,1)S(1)} %pad_maximum_fusion.refs_0_.refs_1_), channel_id=1, source_target_pairs={{0,96},{32,64},{64,32},{96,0},{1,97},{33,65},{65,33},{97,1},{2,98}... | collective-permute-start | bytes 1474568 | tf_op jit(solution)/shard_map/ppermute | solution.py:43
  16.6 29.6 %collective-permute-start.3 = (bf16[160,1536]{1,0:T(8,128)(2,1)S(1)}, bf16[160,1536]{1,0:T(8,128)(2,1)S(1)}, u32[]{:S(2)}, u32[]{:S(2)}) collective-permute-start(bf16[160,1536]{1,0:T(8,128)(2,1)S(1)} %pad_maximum_fusion.refs_0_.refs_1_), channel_id=1, source_target_pairs={{0,64},{32,96},{64,0},{96,32},{1,65},{33,97},{65,1},{97,33},{2,66}... | collective-permute-start | bytes 1474568 | tf_op jit(solution)/shard_map/ppermute | solution.py:43
  55.1 5.8 %collective-permute-start.11 = (f32[32,512]{1,0:T(8,128)S(1)}, f32[32,512]{1,0:T(8,128)S(1)}, u32[]{:S(2)}, u32[]{:S(2)}) collective-permute-start(f32[32,512]{1,0:T(8,128)S(1)} %get-tuple-element.72), channel_id=1, source_target_pairs={{0,1},{1,0},{4,5},{5,4},{2,3},{3,2},{6,7},{7,6},{8,9},{9,8},{12,13... | collective-permute-start | bytes 196616 | tf_op jit(solution)/shard_map/ppermute | solution.py:43
  64.0 8.4 %collective-permute-start.16 = (f32[32,384]{1,0:T(8,128)S(1)}, f32[32,384]{1,0:T(8,128)S(1)}, u32[]{:S(2)}, u32[]{:S(2)}) collective-permute-start(f32[32,384]{1,0:T(8,128)S(1)} %get-tuple-element.75.u0_ref), channel_id=1, source_target_pairs={{0,16},{8,24},{16,0},{24,8},{1,17},{9,25},{17,1},{25,9},{2,18},{10... | collective-permute-start | bytes 147464 | tf_op jit(solution)/shard_map/ppermute | solution.py:43
  66.5 5.9 %collective-permute-start.15 = (f32[32,384]{1,0:T(8,128)S(1)}, f32[32,384]{1,0:T(8,128)S(1)}, u32[]{:S(2)}, u32[]{:S(2)}) collective-permute-start(f32[32,384]{1,0:T(8,128)S(1)} %get-tuple-element.75.u0_ref), channel_id=1, source_target_pairs={{0,24},{8,16},{16,8},{24,0},{1,25},{9,17},{17,9},{25,1},{2,26},{10... | collective-permute-start | bytes 147464 | tf_op jit(solution)/shard_map/ppermute | solution.py:43
  72.4 8.5 %collective-permute-start.19 = (f32[32,1536]{1,0:T(8,128)S(1)}, f32[32,1536]{1,0:T(8,128)S(1)}, u32[]{:S(2)}, u32[]{:S(2)}) collective-permute-start(f32[32,1536]{1,0:T(8,128)S(1)} %constant_dynamic-update-slice_fusion.2.refs_0_.refs_2_), channel_id=1, source_target_pairs={{0,32},{32,0},{64,96},{96,64},{1,33},{33,1},{65,97},{97,65},{2,34}... | collective-permute-start | bytes 589832 | tf_op jit(solution)/shard_map/ppermute | solution.py:43
  72.5 13.0 %collective-permute-start.18 = (f32[32,1536]{1,0:T(8,128)S(1)}, f32[32,1536]{1,0:T(8,128)S(1)}, u32[]{:S(2)}, u32[]{:S(2)}) collective-permute-start(f32[32,1536]{1,0:T(8,128)S(1)} %constant_dynamic-update-slice_fusion.2.refs_0_.refs_2_), channel_id=1, source_target_pairs={{0,96},{32,64},{64,32},{96,0},{1,97},{33,65},{65,33},{97,1},{2,98}... | collective-permute-start | bytes 589832 | tf_op jit(solution)/shard_map/ppermute | solution.py:43
  74.7 15.4 %collective-permute-start.17 = (f32[32,1536]{1,0:T(8,128)S(1)}, f32[32,1536]{1,0:T(8,128)S(1)}, u32[]{:S(2)}, u32[]{:S(2)}) collective-permute-start(f32[32,1536]{1,0:T(8,128)S(1)} %constant_dynamic-update-slice_fusion.2.refs_0_.refs_2_), channel_id=1, source_target_pairs={{0,64},{32,96},{64,0},{96,32},{1,65},{33,97},{65,1},{97,33},{2,66}... | collective-permute-start | bytes 589832 | tf_op jit(solution)/shard_map/ppermute | solution.py:43
  93.8 6.1 %collective-permute-start.21 = (f32[32,512]{1,0:T(8,128)S(1)}, f32[32,512]{1,0:T(8,128)S(1)}, u32[]{:S(2)}, u32[]{:S(2)}) collective-permute-start(f32[32,512]{1,0:T(8,128)S(1)} %get-tuple-element.113), channel_id=1, source_target_pairs={{0,1},{1,0},{4,5},{5,4},{2,3},{3,2},{6,7},{7,6},{8,9},{9,8},{12,13... | collective-permute-start | bytes 196616 | tf_op jit(solution)/shard_map/ppermute | solution.py:43
  95.8 5.5 %collective-permute-start.22 = (f32[32,512]{1,0:T(8,128)S(1)}, f32[32,512]{1,0:T(8,128)S(1)}, u32[]{:S(2)}, u32[]{:S(2)}) collective-permute-start(f32[32,512]{1,0:T(8,128)S(1)} %get-tuple-element.114), channel_id=1, source_target_pairs={{0,5},{1,4},{4,1},{5,0},{2,7},{3,6},{6,3},{7,2},{8,13},{9,12},{12,... | collective-permute-start | bytes 196616 | tf_op jit(solution)/shard_map/ppermute | solution.py:43
  101.4 7.3 %collective-permute-start.26 = (f32[32,384]{1,0:T(8,128)S(1)}, f32[32,384]{1,0:T(8,128)S(1)}, u32[]{:S(2)}, u32[]{:S(2)}) collective-permute-start(f32[32,384]{1,0:T(8,128)S(1)} %get-tuple-element.117.u1_ref), channel_id=1, source_target_pairs={{0,16},{8,24},{16,0},{24,8},{1,17},{9,25},{17,1},{25,9},{2,18},{10... | collective-permute-start | bytes 147464 | tf_op jit(solution)/shard_map/ppermute | solution.py:43
  103.2 5.5 %collective-permute-start.25 = (f32[32,384]{1,0:T(8,128)S(1)}, f32[32,384]{1,0:T(8,128)S(1)}, u32[]{:S(2)}, u32[]{:S(2)}) collective-permute-start(f32[32,384]{1,0:T(8,128)S(1)} %get-tuple-element.117.u1_ref), channel_id=1, source_target_pairs={{0,24},{8,16},{16,8},{24,0},{1,25},{9,17},{17,9},{25,1},{2,26},{10... | collective-permute-start | bytes 147464 | tf_op jit(solution)/shard_map/ppermute | solution.py:43
  108.7 11.1 %collective-permute-start.29 = (f32[32,1536]{1,0:T(8,128)S(1)}, f32[32,1536]{1,0:T(8,128)S(1)}, u32[]{:S(2)}, u32[]{:S(2)}) collective-permute-start(f32[32,1536]{1,0:T(8,128)S(1)} %constant_dynamic-update-slice_fusion.6.refs_0_), channel_id=1, source_target_pairs={{0,32},{32,0},{64,96},{96,64},{1,33},{33,1},{65,97},{97,65},{2,34}... | collective-permute-start | bytes 589832 | tf_op jit(solution)/shard_map/ppermute | solution.py:43
  108.9 15.8 %collective-permute-start.28 = (f32[32,1536]{1,0:T(8,128)S(1)}, f32[32,1536]{1,0:T(8,128)S(1)}, u32[]{:S(2)}, u32[]{:S(2)}) collective-permute-start(f32[32,1536]{1,0:T(8,128)S(1)} %constant_dynamic-update-slice_fusion.6.refs_0_), channel_id=1, source_target_pairs={{0,96},{32,64},{64,32},{96,0},{1,97},{33,65},{65,33},{97,1},{2,98}... | collective-permute-start | bytes 589832 | tf_op jit(solution)/shard_map/ppermute | solution.py:43
  111.0 18.5 %collective-permute-start.27 = (f32[32,1536]{1,0:T(8,128)S(1)}, f32[32,1536]{1,0:T(8,128)S(1)}, u32[]{:S(2)}, u32[]{:S(2)}) collective-permute-start(f32[32,1536]{1,0:T(8,128)S(1)} %constant_dynamic-update-slice_fusion.6.refs_0_), channel_id=1, source_target_pairs={{0,64},{32,96},{64,0},{96,32},{1,65},{33,97},{65,1},{97,33},{2,66}... | collective-permute-start | bytes 589832 | tf_op jit(solution)/shard_map/ppermute | solution.py:43
  134.5 6.1 %collective-permute-start.31 = (f32[32,512]{1,0:T(8,128)S(1)}, f32[32,512]{1,0:T(8,128)S(1)}, u32[]{:S(2)}, u32[]{:S(2)}) collective-permute-start(f32[32,512]{1,0:T(8,128)S(1)} %get-tuple-element.120), channel_id=1, source_target_pairs={{0,1},{1,0},{4,5},{5,4},{2,3},{3,2},{6,7},{7,6},{8,9},{9,8},{12,13... | collective-permute-start | bytes 196616 | tf_op jit(solution)/shard_map/ppermute | solution.py:43
  136.4 5.6 %collective-permute-start.32 = (f32[32,512]{1,0:T(8,128)S(1)}, f32[32,512]{1,0:T(8,128)S(1)}, u32[]{:S(2)}, u32[]{:S(2)}) collective-permute-start(f32[32,512]{1,0:T(8,128)S(1)} %get-tuple-element.121), channel_id=1, source_target_pairs={{0,5},{1,4},{4,1},{5,0},{2,7},{3,6},{6,3},{7,2},{8,13},{9,12},{12,... | collective-permute-start | bytes 196616 | tf_op jit(solution)/shard_map/ppermute | solution.py:43
  (17 other events, 157.7 us)
where the time goes:
time: 166 us; the launch traced here: 163 us
  Pallas kernels  70.2 us (42%)
  starting transfers between devices  46.4 us (28%)
  waiting for transfers between devices  24.1 us (15%)
  blocking collectives  18 us (11%)
  local copies, waits for them, and re-layouts  2.76 us (2%)
    pallas_call x23, Pallas kernels, call(): pl.pallas_call(kernel, out_shape=outs, in_specs=in_specs or [VM] * len(ar...  70.2 us
    ppermute x35, starting transfers between devices, swap(): return lax.ppermute(array, axis, [(i, i ^ k) for i in range(size)])  46.4 us
    ppermute x35, waiting for transfers between devices, swap(): return lax.ppermute(array, axis, [(i, i ^ k) for i in range(size)])  24.1 us
    all_to_all x1, blocking collectives, body(): lax.all_to_all(jnp.broadcast_to(part[None], (64, 8, LANES)), ('x', 'y', *...  18 us
  transfers between devices with their start and end apart: 35, of which 12 were waited for; matrix products, arithmetic and copies ran while one was open for 0% of the time, Pallas kernels for 35%

commit v1 on v0

--- a/solution.py
+++ b/solution.py
@@ -15,7 +15,7 @@
 VM = pl.BlockSpec(memory_space=pltpu.VMEM)
 HB = pl.BlockSpec(memory_space=pltpu.HBM)
 TILE, ROWS, DEPTH = 512, 64, 4
-NEAR, KEEP = (1, 1, 1, 5), 2
+NEAR, KEEP = (1, 1, 1, 4), 2
 FORM_ROOM, APPLY_ROOM = 3 * 2**20, 1 * 2**20
 SIDES, WIDTH, LANES = 32, 384, 128
 

time: 166 us -> 165 us (level)
  local copies, waits for them, and re-layouts: 2.76 us -> 0.23 us
    unnamed x24 -> x28, local copies, waits for them, and re-layouts: 2.66 us -> 0.14 us
where the time goes in v1:
time: 165 us; the launch traced here: 162 us
  Pallas kernels  71.1 us (43%)
  starting transfers between devices  46.4 us (28%)
  waiting for transfers between devices  25 us (15%)
  blocking collectives  18.2 us (11%)
    pallas_call x23, Pallas kernels, call(): pl.pallas_call(kernel, out_shape=outs, in_specs=in_specs or [VM] * len(ar...  71.1 us
    ppermute x35, starting transfers between devices, swap(): return lax.ppermute(array, axis, [(i, i ^ k) for i in range(size)])  46.4 us
    ppermute x35, waiting for transfers between devices, swap(): return lax.ppermute(array, axis, [(i, i ^ k) for i in range(size)])  25 us
    all_to_all x1, blocking collectives, body(): lax.all_to_all(jnp.broadcast_to(part[None], (64, 8, LANES)), ('x', 'y', *...  18.2 us
  transfers between devices with their start and end apart: 35, of which 12 were waited for; matrix products, arithmetic and copies ran while one was open for 0% of the time, Pallas kernels for 35%

profile of v1, /device:TPU:0, one launch (start us, length us, event | category | flops | bytes accessed | tf_op | source)
XLA Modules:
  0.0 162.4 jit_solution(14708560770075889875)
XLA Ops:
  1.6 3.4 %collective-permute-start.2 = (bf16[160,384]{1,0:T(8,128)(2,1)S(1)}, bf16[160,384]{1,0:T(8,128)(2,1)S(1)}, u32[]{:S(2)}, u32[]{:S(2)}) collective-permute-start(bf16[160,384]{1,0:T(8,128)(2,1)S(1)} %pack.1), channel_id=1, source_target_pairs={{0,16},{8,24},{16,0},{24,8},{1,17},{9,25},{17,1},{25,9},{2,18},{10... | collective-permute-start | bytes 368648 | tf_op jit(solution)/shard_map/ppermute | solution.py:43
  6.0 4.1 %collective-permute-start.7 = (bf16[64,768]{1,0:T(8,128)(2,1)S(1)}, bf16[64,768]{1,0:T(8,128)(2,1)S(1)}, u32[]{:S(2)}, u32[]{:S(2)}) collective-permute-start(bf16[64,768]{1,0:T(8,128)(2,1)S(1)} %pad_maximum_fusion.2), channel_id=1, source_target_pairs={{0,5},{1,4},{4,1},{5,0},{2,7},{3,6},{6,3},{7,2},{8,13},{9,12},{12,... | collective-permute-start | bytes 294920 | tf_op jit(solution)/shard_map/ppermute | solution.py:43
  10.2 2.7 %collective-permute-start.5 = (bf16[64,768]{1,0:T(8,128)(2,1)S(1)}, bf16[64,768]{1,0:T(8,128)(2,1)S(1)}, u32[]{:S(2)}, u32[]{:S(2)}) collective-permute-start(bf16[64,768]{1,0:T(8,128)(2,1)S(1)} %pad_maximum_fusion.2), channel_id=1, source_target_pairs={{0,1},{1,0},{4,5},{5,4},{2,3},{3,2},{6,7},{7,6},{8,9},{9,8},{12,13... | collective-permute-start | bytes 294920 | tf_op jit(solution)/shard_map/ppermute | solution.py:43
  16.6 3.0 %collective-permute-start.3 = (bf16[160,1536]{1,0:T(8,128)(2,1)S(1)}, bf16[160,1536]{1,0:T(8,128)(2,1)S(1)}, u32[]{:S(2)}, u32[]{:S(2)}) collective-permute-start(bf16[160,1536]{1,0:T(8,128)(2,1)S(1)} %pad_maximum_fusion.refs_0_.refs_1_), channel_id=1, source_target_pairs={{0,64},{32,96},{64,0},{96,32},{1,65},{33,97},{65,1},{97,33},{2,66}... | collective-permute-start | bytes 1474568 | tf_op jit(solution)/shard_map/ppermute | solution.py:43
  20.1 7.6 %form.4 = (bf16[1536,512]{1,0:T(8,128)(2,1)S(1)}, bf16[1536,512]{1,0:T(8,128)(2,1)S(1)}, bf16[1536,512]{1,0:T(8,128)(2,1)S(1)}, bf16[1536,512]{1,0:T(8,128)(2,1)...) custom-call(bf16[160,1536]{1,0:T(8,128)(2,1)S(1)} %pad_maximum_fusio, ...), custom_call_target="tpu_custom_call" | custom-call | bytes 30600000 | tf_op jit(solution)/shard_map/form/pallas_call | solution.py:26
  27.8 8.0 %form.5 = (bf16[1536,512]{1,0:T(8,128)(2,1)S(1)}, bf16[1536,512]{1,0:T(8,128)(2,1)S(1)}, bf16[1536,512]{1,0:T(8,128)(2,1)S(1)}, bf16[1536,512]{1,0:T(8,128)(2,1)...) custom-call(bf16[160,1536]{1,0:T(8,128)(2,1)S(1)} %collective-permut, ...), custom_call_target="tpu_custom_call" | custom-call | bytes 30600000 | tf_op jit(solution)/shard_map/form/pallas_call | solution.py:26
  35.8 2.7 %collective-permute-done.8.refs_0_.refs_1_ = bf16[160,1536]{1,0:T(8,128)(2,1)S(1)} collective-permute-done((bf16[160,1536]{1,0:T(8,128)(2,1)S(1)}, bf16[160,1536]{1,0:T(8,128)(2,1)S(1)}, u32[]{:S(2)}, u32[]{:S(2)}) %collective-permute-start.8) | collective-permute-done | bytes 491552 | tf_op jit(solution)/shard_map/ppermute | solution.py:43
  38.5 7.6 %form.6 = (bf16[1536,512]{1,0:T(8,128)(2,1)S(1)}, bf16[1536,512]{1,0:T(8,128)(2,1)S(1)}, bf16[1536,512]{1,0:T(8,128)(2,1)S(1)}, bf16[1536,512]{1,0:T(8,128)(2,1)...) custom-call(bf16[160,1536]{1,0:T(8,128)(2,1)S(1)} %collective-permut, ...), custom_call_target="tpu_custom_call" | custom-call | bytes 30600000 | tf_op jit(solution)/shard_map/form/pallas_call | solution.py:26
  46.2 7.2 %form.7 = (bf16[1536,512]{1,0:T(8,128)(2,1)S(1)}, bf16[1536,512]{1,0:T(8,128)(2,1)S(1)}, bf16[1536,512]{1,0:T(8,128)(2,1)S(1)}, bf16[1536,512]{1,0:T(8,128)(2,1)...) custom-call(bf16[160,1536]{1,0:T(8,128)(2,1)S(1)} %collective-permut, ...), custom_call_target="tpu_custom_call" | custom-call | bytes 30600000 | tf_op jit(solution)/shard_map/form/pallas_call | solution.py:26
  55.2 3.3 %collective-permute-start.11 = (f32[32,512]{1,0:T(8,128)S(1)}, f32[32,512]{1,0:T(8,128)S(1)}, u32[]{:S(2)}, u32[]{:S(2)}) collective-permute-start(f32[32,512]{1,0:T(8,128)S(1)} %get-tuple-element.71), channel_id=1, source_target_pairs={{0,1},{1,0},{4,5},{5,4},{2,3},{3,2},{6,7},{7,6},{8,9},{9,8},{12,13... | collective-permute-start | bytes 196616 | tf_op jit(solution)/shard_map/ppermute | solution.py:43
  61.0 3.0 %collective-permute-done.12.m2 = f32[32,512]{1,0:T(8,128)S(1)} collective-permute-done((f32[32,512]{1,0:T(8,128)S(1)}, f32[32,512]{1,0:T(8,128)S(1)}, u32[]{:S(2)}, u32[]{:S(2)}) %collective-permute-start.12) | collective-permute-done | bytes 65568 | tf_op jit(solution)/shard_map/ppermute | solution.py:43
  64.0 2.5 %collective-permute-start.16 = (f32[32,384]{1,0:T(8,128)S(1)}, f32[32,384]{1,0:T(8,128)S(1)}, u32[]{:S(2)}, u32[]{:S(2)}) collective-permute-start(f32[32,384]{1,0:T(8,128)S(1)} %get-tuple-element.74.u0_ref), channel_id=1, source_target_pairs={{0,16},{8,24},{16,0},{24,8},{1,17},{9,25},{17,1},{25,9},{2,18},{10... | collective-permute-start | bytes 147464 | tf_op jit(solution)/shard_map/ppermute | solution.py:43
  68.3 4.1 %collective-permute-done.14 = f32[32,384]{1,0:T(8,128)S(1)} collective-permute-done((f32[32,384]{1,0:T(8,128)S(1)}, f32[32,384]{1,0:T(8,128)S(1)}, u32[]{:S(2)}, u32[]{:S(2)}) %collective-permute-start.14) | collective-permute-done | bytes 49184 | tf_op jit(solution)/shard_map/ppermute | solution.py:43
  76.6 4.3 %apply.10.refs_10_ = f32[32,3200]{1,0:T(8,128)S(1)} custom-call(f32[32,1536]{1,0:T(8,128)S(1)} %constant_dynamic-update-slice_fusion.2.refs_0_.refs_2_, bf16[160,1536]{1,0:T(8,128)(2,1)S(1)} %pad_maximum_fusion.refs_0_.refs_1_, bf16[1536,512]{1,0:T(8,128)(2,1)S(1)} %get-tuple-element.102.refs_2_.refs_4_, ...), custom_call_target="tpu_custom_call" | custom-call | bytes 15840000 | tf_op jit(solution)/shard_map/apply/pallas_call | solution.py:26
  81.0 4.6 %apply.11.refs_10_ = f32[32,3200]{1,0:T(8,128)S(1)} custom-call(f32[32,1536]{1,0:T(8,128)S(1)} %collective-permute-done.19.refs_0_.refs_2_, bf16[160,1536]{1,0:T(8,128)(2,1)S(1)} %collective-permute-done.9.refs_0_.refs_1_, bf16[1536,512]{1,0:T(8,128)(2,1)S(1)} %get-tuple-element.94.refs_2_.refs_4_, bf16[1536,512]{1,0:T(8,128)(2,1)S(1)} %get-tuple-element.95.refs_3_.refs_5_, ...), custom_call_target="tpu_custom_call" | custom-call | bytes 15840000 | tf_op jit(solution)/shard_map/apply/pallas_call | solution.py:26
  85.6 4.6 %apply.12.refs_13_ = f32[32,3200]{1,0:T(8,128)S(1)} custom-call(f32[32,1536]{1,0:T(8,128)S(1)} %collective-permute-done.18.refs_0_.refs_2_, bf16[160,1536]{1,0:T(8,128)(2,1)S(1)} %collective-permute-done.8.refs_0_.refs_1_, bf16[1536,512]{1,0:T(8,128)(2,1)S(1)} %get-tuple-element.86.refs_2_.refs_4_, bf16[1536,512]{1,0:T(8,128)(2,1)S(1)} %get-tuple-element.87.refs_3_.refs_5_, ...), custom_call_target="tpu_custom_call" | custom-call | bytes 15840000 | tf_op jit(solution)/shard_map/apply/pallas_call | solution.py:26
  90.2 2.5 %apply.13.refs_14_ = f32[32,1664]{1,0:T(8,128)S(1)} custom-call(f32[32,1536]{1,0:T(8,128)S(1)} %collective-permute-done.17.refs_0_.refs_2_, bf16[160,1536]{1,0:T(8,128)(2,1)S(1)} %collective-permute-done.3.refs_0_.refs_1_, bf16[1536,512]{1,0:T(8,128)(2,1)S(1)} %get-tuple-element.75.refs_2_.refs_4_, bf16[1536,512]{1,0:T(8,128)(2,1)S(1)} %get-tuple-element.76.refs_3_.refs_5_, ...), custom_call_target="tpu_custom_call" | custom-call | bytes 7920000 | tf_op jit(solution)/shard_map/apply/pallas_call | solution.py:26
  106.0 3.3 %collective-permute-done.24 = f32[32,384]{1,0:T(8,128)S(1)} collective-permute-done((f32[32,384]{1,0:T(8,128)S(1)}, f32[32,384]{1,0:T(8,128)S(1)}, u32[]{:S(2)}, u32[]{:S(2)}) %collective-permute-start.24) | collective-permute-done | bytes 49184 | tf_op jit(solution)/shard_map/ppermute | solution.py:43
  113.5 5.5 %apply.15.refs_12_ = f32[32,3200]{1,0:T(8,128)S(1)} custom-call(f32[32,1536]{1,0:T(8,128)S(1)} %constant_dynamic-update-slice_fusion.6.refs_0_, bf16[160,1536]{1,0:T(8,128)(2,1)S(1)} %pad_maximum_fusion.refs_0_.refs_1_, f32[32,1536]{1,0:T(8,128)S(1)} %constant_dynamic-update-slice_fusion.2.refs_0_.refs_2_, ...), custom_call_target="tpu_custom_call" | custom-call | bytes 15840000 | tf_op jit(solution)/shard_map/apply/pallas_call | solution.py:26
  119.0 4.8 %apply.16.refs_12_ = f32[32,3200]{1,0:T(8,128)S(1)} custom-call(f32[32,1536]{1,0:T(8,128)S(1)} %collective-permute-done.29.refs_0_, bf16[160,1536]{1,0:T(8,128)(2,1)S(1)} %collective-permute-done.9.refs_0_.refs_1_, f32[32,1536]{1,0:T(8,128)S(1)} %copy-done.5, f32[32,128]{1,0:T(8,128)S(1)} %get-tuple-element.116.refs_3_.coef_ref, ...), custom_call_target="tpu_custom_call" | custom-call | bytes 15840000 | tf_op jit(solution)/shard_map/apply/pallas_call | solution.py:26
  123.9 4.8 %apply.17.refs_15_ = f32[32,3200]{1,0:T(8,128)S(1)} custom-call(f32[32,1536]{1,0:T(8,128)S(1)} %collective-permute-done.28.refs_0_, bf16[160,1536]{1,0:T(8,128)(2,1)S(1)} %collective-permute-done.8.refs_0_.refs_1_, f32[32,1536]{1,0:T(8,128)S(1)} %collective-permute-done.18.refs_0_.refs_2_, f32[32,128]{1,0:T(8,128)S(1)} %get-tuple-element.116.refs_3_.coef_ref, ...), custom_call_target="tpu_custom_call" | custom-call | bytes 15840000 | tf_op jit(solution)/shard_map/apply/pallas_call | solution.py:26
  128.7 3.3 %apply.18.refs_16_ = f32[32,1664]{1,0:T(8,128)S(1)} custom-call(f32[32,1536]{1,0:T(8,128)S(1)} %collective-permute-done.27.refs_0_, bf16[160,1536]{1,0:T(8,128)(2,1)S(1)} %collective-permute-done.3.refs_0_.refs_1_, f32[32,1536]{1,0:T(8,128)S(1)} %collective-permute-done.17.refs_0_.refs_2_, f32[32,128]{1,0:T(8,128)S(1)} %get-tuple-element.116.refs_3_.coef_ref, ...), custom_call_target="tpu_custom_call" | custom-call | bytes 7920000 | tf_op jit(solution)/shard_map/apply/pallas_call | solution.py:26
  137.4 2.5 %collective-permute-done.31.m1 = f32[32,512]{1,0:T(8,128)S(1)} collective-permute-done((f32[32,512]{1,0:T(8,128)S(1)}, f32[32,512]{1,0:T(8,128)S(1)}, u32[]{:S(2)}, u32[]{:S(2)}) %collective-permute-start.31) | collective-permute-done | bytes 65568 | tf_op jit(solution)/shard_map/ppermute | solution.py:43
  142.9 18.2 %all_to_all.5.sums_ref = f32[64,8,128]{2,1,0:T(8,128)S(1)} all-to-all(f32[64,8,128]{2,1,0:T(8,128)S(1)} %broadcast_in_dim.2), channel_id=1, replica_groups=mesh['x'=4,'y'=4,'zl'=2,'c'=2,'zh'=2] {'x','y','zl','zh'}, dimensions={0} | all-to-all | bytes 524288 | tf_op jit(solution)/shard_map/all_to_all | solution.py:428
  (110 shorter events, 43.2 us)
Async XLA Ops:
  1.6 8.6 %collective-permute-start.2 = (bf16[160,384]{1,0:T(8,128)(2,1)S(1)}, bf16[160,384]{1,0:T(8,128)(2,1)S(1)}, u32[]{:S(2)}, u32[]{:S(2)}) collective-permute-start(bf16[160,384]{1,0:T(8,128)(2,1)S(1)} %pack.1), channel_id=1, source_target_pairs={{0,16},{8,24},{16,0},{24,8},{1,17},{9,25},{17,1},{25,9},{2,18},{10... | collective-permute-start | bytes 368648 | tf_op jit(solution)/shard_map/ppermute | solution.py:43
  4.9 7.9 %collective-permute-start.1 = (bf16[160,384]{1,0:T(8,128)(2,1)S(1)}, bf16[160,384]{1,0:T(8,128)(2,1)S(1)}, u32[]{:S(2)}, u32[]{:S(2)}) collective-permute-start(bf16[160,384]{1,0:T(8,128)(2,1)S(1)} %pack.1), channel_id=1, source_target_pairs={{0,24},{8,16},{16,8},{24,0},{1,25},{9,17},{17,9},{25,1},{2,26},{10... | collective-permute-start | bytes 368648 | tf_op jit(solution)/shard_map/ppermute | solution.py:43
  6.0 6.9 %collective-permute-start = (bf16[160,384]{1,0:T(8,128)(2,1)S(1)}, bf16[160,384]{1,0:T(8,128)(2,1)S(1)}, u32[]{:S(2)}, u32[]{:S(2)}) collective-permute-start(bf16[160,384]{1,0:T(8,128)(2,1)S(1)} %pack.1), channel_id=1, source_target_pairs={{0,8},{8,0},{16,24},{24,16},{1,9},{9,1},{17,25},{25,17},{2,10},{10... | collective-permute-start | bytes 368648 | tf_op jit(solution)/shard_map/ppermute | solution.py:43
  6.0 13.6 %collective-permute-start.7 = (bf16[64,768]{1,0:T(8,128)(2,1)S(1)}, bf16[64,768]{1,0:T(8,128)(2,1)S(1)}, u32[]{:S(2)}, u32[]{:S(2)}) collective-permute-start(bf16[64,768]{1,0:T(8,128)(2,1)S(1)} %pad_maximum_fusion.2), channel_id=1, source_target_pairs={{0,5},{1,4},{4,1},{5,0},{2,7},{3,6},{6,3},{7,2},{8,13},{9,12},{12,... | collective-permute-start | bytes 294920 | tf_op jit(solution)/shard_map/ppermute | solution.py:43
  10.2 9.5 %collective-permute-start.6 = (bf16[64,768]{1,0:T(8,128)(2,1)S(1)}, bf16[64,768]{1,0:T(8,128)(2,1)S(1)}, u32[]{:S(2)}, u32[]{:S(2)}) collective-permute-start(bf16[64,768]{1,0:T(8,128)(2,1)S(1)} %pad_maximum_fusion.2), channel_id=1, source_target_pairs={{0,4},{1,5},{4,0},{5,1},{2,6},{3,7},{6,2},{7,3},{8,12},{9,13},{12,... | collective-permute-start | bytes 294920 | tf_op jit(solution)/shard_map/ppermute | solution.py:43
  10.2 6.4 %collective-permute-start.5 = (bf16[64,768]{1,0:T(8,128)(2,1)S(1)}, bf16[64,768]{1,0:T(8,128)(2,1)S(1)}, u32[]{:S(2)}, u32[]{:S(2)}) collective-permute-start(bf16[64,768]{1,0:T(8,128)(2,1)S(1)} %pad_maximum_fusion.2), channel_id=1, source_target_pairs={{0,1},{1,0},{4,5},{5,4},{2,3},{3,2},{6,7},{7,6},{8,9},{9,8},{12,13... | collective-permute-start | bytes 294920 | tf_op jit(solution)/shard_map/ppermute | solution.py:43
  12.9 14.9 %collective-permute-start.9 = (bf16[160,1536]{1,0:T(8,128)(2,1)S(1)}, bf16[160,1536]{1,0:T(8,128)(2,1)S(1)}, u32[]{:S(2)}, u32[]{:S(2)}) collective-permute-start(bf16[160,1536]{1,0:T(8,128)(2,1)S(1)} %pad_maximum_fusion.refs_0_.refs_1_), channel_id=1, source_target_pairs={{0,32},{32,0},{64,96},{96,64},{1,33},{33,1},{65,97},{97,65},{2,34}... | collective-permute-start | bytes 1474568 | tf_op jit(solution)/shard_map/ppermute | solution.py:43
  14.5 24.0 %collective-permute-start.8 = (bf16[160,1536]{1,0:T(8,128)(2,1)S(1)}, bf16[160,1536]{1,0:T(8,128)(2,1)S(1)}, u32[]{:S(2)}, u32[]{:S(2)}) collective-permute-start(bf16[160,1536]{1,0:T(8,128)(2,1)S(1)} %pad_maximum_fusion.refs_0_.refs_1_), channel_id=1, source_target_pairs={{0,96},{32,64},{64,32},{96,0},{1,97},{33,65},{65,33},{97,1},{2,98}... | collective-permute-start | bytes 1474568 | tf_op jit(solution)/shard_map/ppermute | solution.py:43
  16.6 29.6 %collective-permute-start.3 = (bf16[160,1536]{1,0:T(8,128)(2,1)S(1)}, bf16[160,1536]{1,0:T(8,128)(2,1)S(1)}, u32[]{:S(2)}, u32[]{:S(2)}) collective-permute-start(bf16[160,1536]{1,0:T(8,128)(2,1)S(1)} %pad_maximum_fusion.refs_0_.refs_1_), channel_id=1, source_target_pairs={{0,64},{32,96},{64,0},{96,32},{1,65},{33,97},{65,1},{97,33},{2,66}... | collective-permute-start | bytes 1474568 | tf_op jit(solution)/shard_map/ppermute | solution.py:43
  55.2 5.8 %collective-permute-start.11 = (f32[32,512]{1,0:T(8,128)S(1)}, f32[32,512]{1,0:T(8,128)S(1)}, u32[]{:S(2)}, u32[]{:S(2)}) collective-permute-start(f32[32,512]{1,0:T(8,128)S(1)} %get-tuple-element.71), channel_id=1, source_target_pairs={{0,1},{1,0},{4,5},{5,4},{2,3},{3,2},{6,7},{7,6},{8,9},{9,8},{12,13... | collective-permute-start | bytes 196616 | tf_op jit(solution)/shard_map/ppermute | solution.py:43
  58.5 5.5 %collective-permute-start.12 = (f32[32,512]{1,0:T(8,128)S(1)}, f32[32,512]{1,0:T(8,128)S(1)}, u32[]{:S(2)}, u32[]{:S(2)}) collective-permute-start(f32[32,512]{1,0:T(8,128)S(1)} %get-tuple-element.72), channel_id=1, source_target_pairs={{0,5},{1,4},{4,1},{5,0},{2,7},{3,6},{6,3},{7,2},{8,13},{9,12},{12,... | collective-permute-start | bytes 196616 | tf_op jit(solution)/shard_map/ppermute | solution.py:43
  64.0 8.4 %collective-permute-start.16 = (f32[32,384]{1,0:T(8,128)S(1)}, f32[32,384]{1,0:T(8,128)S(1)}, u32[]{:S(2)}, u32[]{:S(2)}) collective-permute-start(f32[32,384]{1,0:T(8,128)S(1)} %get-tuple-element.74.u0_ref), channel_id=1, source_target_pairs={{0,16},{8,24},{16,0},{24,8},{1,17},{9,25},{17,1},{25,9},{2,18},{10... | collective-permute-start | bytes 147464 | tf_op jit(solution)/shard_map/ppermute | solution.py:43
  66.5 5.9 %collective-permute-start.15 = (f32[32,384]{1,0:T(8,128)S(1)}, f32[32,384]{1,0:T(8,128)S(1)}, u32[]{:S(2)}, u32[]{:S(2)}) collective-permute-start(f32[32,384]{1,0:T(8,128)S(1)} %get-tuple-element.74.u0_ref), channel_id=1, source_target_pairs={{0,24},{8,16},{16,8},{24,0},{1,25},{9,17},{17,9},{25,1},{2,26},{10... | collective-permute-start | bytes 147464 | tf_op jit(solution)/shard_map/ppermute | solution.py:43
  72.4 8.5 %collective-permute-start.19 = (f32[32,1536]{1,0:T(8,128)S(1)}, f32[32,1536]{1,0:T(8,128)S(1)}, u32[]{:S(2)}, u32[]{:S(2)}) collective-permute-start(f32[32,1536]{1,0:T(8,128)S(1)} %constant_dynamic-update-slice_fusion.2.refs_0_.refs_2_), channel_id=1, source_target_pairs={{0,32},{32,0},{64,96},{96,64},{1,33},{33,1},{65,97},{97,65},{2,34}... | collective-permute-start | bytes 589832 | tf_op jit(solution)/shard_map/ppermute | solution.py:43
  72.5 13.1 %collective-permute-start.18 = (f32[32,1536]{1,0:T(8,128)S(1)}, f32[32,1536]{1,0:T(8,128)S(1)}, u32[]{:S(2)}, u32[]{:S(2)}) collective-permute-start(f32[32,1536]{1,0:T(8,128)S(1)} %constant_dynamic-update-slice_fusion.2.refs_0_.refs_2_), channel_id=1, source_target_pairs={{0,96},{32,64},{64,32},{96,0},{1,97},{33,65},{65,33},{97,1},{2,98}... | collective-permute-start | bytes 589832 | tf_op jit(solution)/shard_map/ppermute | solution.py:43
  74.7 15.5 %collective-permute-start.17 = (f32[32,1536]{1,0:T(8,128)S(1)}, f32[32,1536]{1,0:T(8,128)S(1)}, u32[]{:S(2)}, u32[]{:S(2)}) collective-permute-start(f32[32,1536]{1,0:T(8,128)S(1)} %constant_dynamic-update-slice_fusion.2.refs_0_.refs_2_), channel_id=1, source_target_pairs={{0,64},{32,96},{64,0},{96,32},{1,65},{33,97},{65,1},{97,33},{2,66}... | collective-permute-start | bytes 589832 | tf_op jit(solution)/shard_map/ppermute | solution.py:43
  94.6 6.1 %collective-permute-start.21 = (f32[32,512]{1,0:T(8,128)S(1)}, f32[32,512]{1,0:T(8,128)S(1)}, u32[]{:S(2)}, u32[]{:S(2)}) collective-permute-start(f32[32,512]{1,0:T(8,128)S(1)} %get-tuple-element.111), channel_id=1, source_target_pairs={{0,1},{1,0},{4,5},{5,4},{2,3},{3,2},{6,7},{7,6},{8,9},{9,8},{12,13... | collective-permute-start | bytes 196616 | tf_op jit(solution)/shard_map/ppermute | solution.py:43
  96.6 5.5 %collective-permute-start.22 = (f32[32,512]{1,0:T(8,128)S(1)}, f32[32,512]{1,0:T(8,128)S(1)}, u32[]{:S(2)}, u32[]{:S(2)}) collective-permute-start(f32[32,512]{1,0:T(8,128)S(1)} %get-tuple-element.112), channel_id=1, source_target_pairs={{0,5},{1,4},{4,1},{5,0},{2,7},{3,6},{6,3},{7,2},{8,13},{9,12},{12,... | collective-permute-start | bytes 196616 | tf_op jit(solution)/shard_map/ppermute | solution.py:43
  102.2 7.1 %collective-permute-start.26 = (f32[32,384]{1,0:T(8,128)S(1)}, f32[32,384]{1,0:T(8,128)S(1)}, u32[]{:S(2)}, u32[]{:S(2)}) collective-permute-start(f32[32,384]{1,0:T(8,128)S(1)} %get-tuple-element.115.u1_ref), channel_id=1, source_target_pairs={{0,16},{8,24},{16,0},{24,8},{1,17},{9,25},{17,1},{25,9},{2,18},{10... | collective-permute-start | bytes 147464 | tf_op jit(solution)/shard_map/ppermute | solution.py:43
  109.3 9.7 %collective-permute-start.29 = (f32[32,1536]{1,0:T(8,128)S(1)}, f32[32,1536]{1,0:T(8,128)S(1)}, u32[]{:S(2)}, u32[]{:S(2)}) collective-permute-start(f32[32,1536]{1,0:T(8,128)S(1)} %constant_dynamic-update-slice_fusion.6.refs_0_), channel_id=1, source_target_pairs={{0,32},{32,0},{64,96},{96,64},{1,33},{33,1},{65,97},{97,65},{2,34}... | collective-permute-start | bytes 589832 | tf_op jit(solution)/shard_map/ppermute | solution.py:43
  109.5 14.4 %collective-permute-start.28 = (f32[32,1536]{1,0:T(8,128)S(1)}, f32[32,1536]{1,0:T(8,128)S(1)}, u32[]{:S(2)}, u32[]{:S(2)}) collective-permute-start(f32[32,1536]{1,0:T(8,128)S(1)} %constant_dynamic-update-slice_fusion.6.refs_0_), channel_id=1, source_target_pairs={{0,96},{32,64},{64,32},{96,0},{1,97},{33,65},{65,33},{97,1},{2,98}... | collective-permute-start | bytes 589832 | tf_op jit(solution)/shard_map/ppermute | solution.py:43
  111.6 17.1 %collective-permute-start.27 = (f32[32,1536]{1,0:T(8,128)S(1)}, f32[32,1536]{1,0:T(8,128)S(1)}, u32[]{:S(2)}, u32[]{:S(2)}) collective-permute-start(f32[32,1536]{1,0:T(8,128)S(1)} %constant_dynamic-update-slice_fusion.6.refs_0_), channel_id=1, source_target_pairs={{0,64},{32,96},{64,0},{96,32},{1,65},{33,97},{65,1},{97,33},{2,66}... | collective-permute-start | bytes 589832 | tf_op jit(solution)/shard_map/ppermute | solution.py:43
  133.8 6.1 %collective-permute-start.31 = (f32[32,512]{1,0:T(8,128)S(1)}, f32[32,512]{1,0:T(8,128)S(1)}, u32[]{:S(2)}, u32[]{:S(2)}) collective-permute-start(f32[32,512]{1,0:T(8,128)S(1)} %get-tuple-element.118), channel_id=1, source_target_pairs={{0,1},{1,0},{4,5},{5,4},{2,3},{3,2},{6,7},{7,6},{8,9},{9,8},{12,13... | collective-permute-start | bytes 196616 | tf_op jit(solution)/shard_map/ppermute | solution.py:43
  135.8 5.5 %collective-permute-start.32 = (f32[32,512]{1,0:T(8,128)S(1)}, f32[32,512]{1,0:T(8,128)S(1)}, u32[]{:S(2)}, u32[]{:S(2)}) collective-permute-start(f32[32,512]{1,0:T(8,128)S(1)} %get-tuple-element.119), channel_id=1, source_target_pairs={{0,5},{1,4},{4,1},{5,0},{2,7},{3,6},{6,3},{7,2},{8,13},{9,12},{12,... | collective-permute-start | bytes 196616 | tf_op jit(solution)/shard_map/ppermute | solution.py:43
  (19 other events, 233.6 us)

commit v2 on v1

--- a/solution.py
+++ b/solution.py
@@ -115,7 +115,7 @@
     def copy(c, slot):
         return pltpu.make_async_copy(stage.at[slot], far_ref.at[c - near], sems.at[slot])
 
-    def step(units, c, slot):
+    def step(units, c, slot, earlier):
         starts = [pl.multiple_of(c * TILE + m * 256, 256) for m in range(2)]
         lows = near_refs[c] if slot is None else stage.at[slot]
 
@@ -125,23 +125,37 @@
             hi_refs[c][at, m * 256 : m * 256 + 256] = high
             lows[at, m * 256 : m * 256 + 256] = (value - high.astype(F32)).astype(BF16)
 
-        for m in range(2):
-            pltpu.matmul_push_rhs(right[:, pl.ds(starts[m], 256)], 0, m)
         waiting = []
+        groups, turn = 3, 0
         for r in range(count // ROWS):
+            fresh = r % (count // ROWS // groups) == 0
+            if fresh:
+                if r and earlier is not None:
+                    multiply(units, *earlier, turn)
+                    turn += 1
+                if r == 0 or earlier is not None:
+                    for m in range(2):
+                        pltpu.matmul_push_rhs(right[:, pl.ds(starts[m], 256)], 0, m)
+            load = 0 if r == 0 or (fresh and earlier is not None) else None
             at = slice(r * ROWS, r * ROWS + ROWS)
             for m in range(2):
                 unit = units[m][r % DEPTH]
-                pltpu.matmul_acc_lhs(unit, left[at, :], load_staged_rhs=0 if r == 0 else None)
+                pltpu.matmul_acc_lhs(unit, left[at, :], load_staged_rhs=load)
                 waiting.append((at, m, unit))
             if len(waiting) > 2 * (DEPTH - 1):
                 for _ in range(2):
                     at, m, unit = waiting.pop(0)
                     finish(at, m, pltpu.matmul_pop(unit))
+        if earlier is not None:
+            multiply(units, *earlier, turn)
+            store(units, earlier[0])
         for at, m, unit in waiting:
             finish(at, m, pltpu.matmul_pop(unit))
-        turn = 0
-        for k in range(count // 256):
+        return c, lows
+
+    def multiply(units, c, lows, part):
+        turn, each = 0, count // 256 // 3
+        for k in range(part * each, part * each + each):
             rows = slice(k * 256, k * 256 + 256)
             for source, which, height in ((hi_refs[c], -2, 96), (lows, -1, 64)):
                 for m in range(2):
@@ -149,24 +163,31 @@
                 for m in range(2):
                     pltpu.matmul_acc_lhs(units[m][which], pack_ref[64 : 64 + height, rows], load_staged_rhs=turn % 2)
                 turn += 1
+
+    def store(units, c):
         for m in range(2):
+            cols = slice(c * TILE + m * 256, c * TILE + m * 256 + 256)
             a, b = pltpu.matmul_pop(units[m][-2]), pltpu.matmul_pop(units[m][-1])
             value = a[0:SIDES] + (a[SIDES : 2 * SIDES] + ((b[0:SIDES] + b[SIDES:]) + a[2 * SIDES :]))
             if acc_ref is not None:
-                value = value + acc_ref[:, pl.ds(starts[m], 256)]
-            out_ref[:, pl.ds(starts[m], 256)] = value
+                value = value + acc_ref[:, cols]
+            out_ref[:, cols] = value
 
     def steps(*units):
         each = len(units) // 2
         units = (units[:each], units[each:])
+        earlier = None
         for c in range(near, tiles):
             slot = (c - near) % KEEP
             if c >= near + KEEP:
                 copy(c - KEEP, slot).wait()
-            step(units, c, slot)
+            earlier = step(units, c, slot, earlier)
             copy(c, slot).start()
         for c in range(near):
-            step(units, c, None)
+            earlier = step(units, c, None, earlier)
+        for part in range(3):
+            multiply(units, *earlier, part)
+        store(units, earlier[0])
         for c in range(max(near, tiles - KEEP), tiles):
             copy(c, (c - near) % KEEP).wait()
 

time: 165 us -> 166 us (level)
  transfers between devices with their start and end apart: 35 -> 35, of which waited for: 12 -> 12; matrix products, arithmetic and copies ran while one was open for 0% -> 0% of each run, Pallas kernels for 35% -> 34%
where the time goes in v2:
time: 166 us; the launch traced here: 163 us
  Pallas kernels  70.3 us (42%)
  starting transfers between devices  46.7 us (28%)
  waiting for transfers between devices  25.8 us (16%)
  blocking collectives  18 us (11%)
    pallas_call x23, Pallas kernels, call(): pl.pallas_call(kernel, out_shape=outs, in_specs=in_specs or [VM] * len(ar...  70.3 us
    ppermute x35, starting transfers between devices, swap(): return lax.ppermute(array, axis, [(i, i ^ k) for i in range(size)])  46.7 us
    ppermute x35, waiting for transfers between devices, swap(): return lax.ppermute(array, axis, [(i, i ^ k) for i in range(size)])  25.8 us
    all_to_all x1, blocking collectives, body(): lax.all_to_all(jnp.broadcast_to(part[None], (64, 8, LANES)), ('x', 'y', *...  18 us
  transfers between devices with their start and end apart: 35, of which 12 were waited for; matrix products, arithmetic and copies ran while one was open for 0% of the time, Pallas kernels for 34%

profile of v2, /device:TPU:0, one launch (start us, length us, event | category | flops | bytes accessed | tf_op | source)
XLA Modules:
  0.0 162.8 jit_solution(3842319079426775379)
XLA Ops:
  1.6 3.4 %collective-permute-start.2 = (bf16[160,384]{1,0:T(8,128)(2,1)S(1)}, bf16[160,384]{1,0:T(8,128)(2,1)S(1)}, u32[]{:S(2)}, u32[]{:S(2)}) collective-permute-start(bf16[160,384]{1,0:T(8,128)(2,1)S(1)} %pack.1), channel_id=1, source_target_pairs={{0,16},{8,24},{16,0},{24,8},{1,17},{9,25},{17,1},{25,9},{2,18},{10... | collective-permute-start | bytes 368648 | tf_op jit(solution)/shard_map/ppermute | solution.py:43
  6.0 4.1 %collective-permute-start.7 = (bf16[64,768]{1,0:T(8,128)(2,1)S(1)}, bf16[64,768]{1,0:T(8,128)(2,1)S(1)}, u32[]{:S(2)}, u32[]{:S(2)}) collective-permute-start(bf16[64,768]{1,0:T(8,128)(2,1)S(1)} %pad_maximum_fusion.2), channel_id=1, source_target_pairs={{0,5},{1,4},{4,1},{5,0},{2,7},{3,6},{6,3},{7,2},{8,13},{9,12},{12,... | collective-permute-start | bytes 294920 | tf_op jit(solution)/shard_map/ppermute | solution.py:43
  10.2 2.7 %collective-permute-start.5 = (bf16[64,768]{1,0:T(8,128)(2,1)S(1)}, bf16[64,768]{1,0:T(8,128)(2,1)S(1)}, u32[]{:S(2)}, u32[]{:S(2)}) collective-permute-start(bf16[64,768]{1,0:T(8,128)(2,1)S(1)} %pad_maximum_fusion.2), channel_id=1, source_target_pairs={{0,1},{1,0},{4,5},{5,4},{2,3},{3,2},{6,7},{7,6},{8,9},{9,8},{12,13... | collective-permute-start | bytes 294920 | tf_op jit(solution)/shard_map/ppermute | solution.py:43
  16.6 3.3 %collective-permute-start.3 = (bf16[160,1536]{1,0:T(8,128)(2,1)S(1)}, bf16[160,1536]{1,0:T(8,128)(2,1)S(1)}, u32[]{:S(2)}, u32[]{:S(2)}) collective-permute-start(bf16[160,1536]{1,0:T(8,128)(2,1)S(1)} %pad_maximum_fusion.refs_0_.refs_1_), channel_id=1, source_target_pairs={{0,64},{32,96},{64,0},{96,32},{1,65},{33,97},{65,1},{97,33},{2,66}... | collective-permute-start | bytes 1474568 | tf_op jit(solution)/shard_map/ppermute | solution.py:43
  20.4 7.3 %form.4 = (bf16[1536,512]{1,0:T(8,128)(2,1)S(1)}, bf16[1536,512]{1,0:T(8,128)(2,1)S(1)}, bf16[1536,512]{1,0:T(8,128)(2,1)S(1)}, bf16[1536,512]{1,0:T(8,128)(2,1)...) custom-call(bf16[160,1536]{1,0:T(8,128)(2,1)S(1)} %pad_maximum_fusio, ...), custom_call_target="tpu_custom_call" | custom-call | bytes 30600000 | tf_op jit(solution)/shard_map/form/pallas_call | solution.py:26
  27.7 7.4 %form.5 = (bf16[1536,512]{1,0:T(8,128)(2,1)S(1)}, bf16[1536,512]{1,0:T(8,128)(2,1)S(1)}, bf16[1536,512]{1,0:T(8,128)(2,1)S(1)}, bf16[1536,512]{1,0:T(8,128)(2,1)...) custom-call(bf16[160,1536]{1,0:T(8,128)(2,1)S(1)} %collective-permut, ...), custom_call_target="tpu_custom_call" | custom-call | bytes 30600000 | tf_op jit(solution)/shard_map/form/pallas_call | solution.py:26
  35.2 3.3 %collective-permute-done.8.refs_0_.refs_1_ = bf16[160,1536]{1,0:T(8,128)(2,1)S(1)} collective-permute-done((bf16[160,1536]{1,0:T(8,128)(2,1)S(1)}, bf16[160,1536]{1,0:T(8,128)(2,1)S(1)}, u32[]{:S(2)}, u32[]{:S(2)}) %collective-permute-start.8) | collective-permute-done | bytes 491552 | tf_op jit(solution)/shard_map/ppermute | solution.py:43
  38.5 7.4 %form.6 = (bf16[1536,512]{1,0:T(8,128)(2,1)S(1)}, bf16[1536,512]{1,0:T(8,128)(2,1)S(1)}, bf16[1536,512]{1,0:T(8,128)(2,1)S(1)}, bf16[1536,512]{1,0:T(8,128)(2,1)...) custom-call(bf16[160,1536]{1,0:T(8,128)(2,1)S(1)} %collective-permut, ...), custom_call_target="tpu_custom_call" | custom-call | bytes 30600000 | tf_op jit(solution)/shard_map/form/pallas_call | solution.py:26
  46.0 7.5 %form.7 = (bf16[1536,512]{1,0:T(8,128)(2,1)S(1)}, bf16[1536,512]{1,0:T(8,128)(2,1)S(1)}, bf16[1536,512]{1,0:T(8,128)(2,1)S(1)}, bf16[1536,512]{1,0:T(8,128)(2,1)...) custom-call(bf16[160,1536]{1,0:T(8,128)(2,1)S(1)} %collective-permut, ...), custom_call_target="tpu_custom_call" | custom-call | bytes 30600000 | tf_op jit(solution)/shard_map/form/pallas_call | solution.py:26
  55.2 3.3 %collective-permute-start.11 = (f32[32,512]{1,0:T(8,128)S(1)}, f32[32,512]{1,0:T(8,128)S(1)}, u32[]{:S(2)}, u32[]{:S(2)}) collective-permute-start(f32[32,512]{1,0:T(8,128)S(1)} %get-tuple-element.71), channel_id=1, source_target_pairs={{0,1},{1,0},{4,5},{5,4},{2,3},{3,2},{6,7},{7,6},{8,9},{9,8},{12,13... | collective-permute-start | bytes 196616 | tf_op jit(solution)/shard_map/ppermute | solution.py:43
  61.0 2.9 %collective-permute-done.12.m2 = f32[32,512]{1,0:T(8,128)S(1)} collective-permute-done((f32[32,512]{1,0:T(8,128)S(1)}, f32[32,512]{1,0:T(8,128)S(1)}, u32[]{:S(2)}, u32[]{:S(2)}) %collective-permute-start.12) | collective-permute-done | bytes 65568 | tf_op jit(solution)/shard_map/ppermute | solution.py:43
  64.0 2.6 %collective-permute-start.16 = (f32[32,384]{1,0:T(8,128)S(1)}, f32[32,384]{1,0:T(8,128)S(1)}, u32[]{:S(2)}, u32[]{:S(2)}) collective-permute-start(f32[32,384]{1,0:T(8,128)S(1)} %get-tuple-element.74.u0_ref), channel_id=1, source_target_pairs={{0,16},{8,24},{16,0},{24,8},{1,17},{9,25},{17,1},{25,9},{2,18},{10... | collective-permute-start | bytes 147464 | tf_op jit(solution)/shard_map/ppermute | solution.py:43
  68.3 4.1 %collective-permute-done.14 = f32[32,384]{1,0:T(8,128)S(1)} collective-permute-done((f32[32,384]{1,0:T(8,128)S(1)}, f32[32,384]{1,0:T(8,128)S(1)}, u32[]{:S(2)}, u32[]{:S(2)}) %collective-permute-start.14) | collective-permute-done | bytes 49184 | tf_op jit(solution)/shard_map/ppermute | solution.py:43
  76.8 4.3 %apply.10.refs_10_ = f32[32,3200]{1,0:T(8,128)S(1)} custom-call(f32[32,1536]{1,0:T(8,128)S(1)} %constant_dynamic-update-slice_fusion.2.refs_0_.refs_2_, bf16[160,1536]{1,0:T(8,128)(2,1)S(1)} %pad_maximum_fusion.refs_0_.refs_1_, bf16[1536,512]{1,0:T(8,128)(2,1)S(1)} %get-tuple-element.102.refs_2_.refs_4_, ...), custom_call_target="tpu_custom_call" | custom-call | bytes 15840000 | tf_op jit(solution)/shard_map/apply/pallas_call | solution.py:26
  81.2 4.6 %apply.11.refs_10_ = f32[32,3200]{1,0:T(8,128)S(1)} custom-call(f32[32,1536]{1,0:T(8,128)S(1)} %collective-permute-done.19.refs_0_.refs_2_, bf16[160,1536]{1,0:T(8,128)(2,1)S(1)} %collective-permute-done.9.refs_0_.refs_1_, bf16[1536,512]{1,0:T(8,128)(2,1)S(1)} %get-tuple-element.94.refs_2_.refs_4_, bf16[1536,512]{1,0:T(8,128)(2,1)S(1)} %get-tuple-element.95.refs_3_.refs_5_, ...), custom_call_target="tpu_custom_call" | custom-call | bytes 15840000 | tf_op jit(solution)/shard_map/apply/pallas_call | solution.py:26
  85.8 4.6 %apply.12.refs_13_ = f32[32,3200]{1,0:T(8,128)S(1)} custom-call(f32[32,1536]{1,0:T(8,128)S(1)} %collective-permute-done.18.refs_0_.refs_2_, bf16[160,1536]{1,0:T(8,128)(2,1)S(1)} %collective-permute-done.8.refs_0_.refs_1_, bf16[1536,512]{1,0:T(8,128)(2,1)S(1)} %get-tuple-element.86.refs_2_.refs_4_, bf16[1536,512]{1,0:T(8,128)(2,1)S(1)} %get-tuple-element.87.refs_3_.refs_5_, ...), custom_call_target="tpu_custom_call" | custom-call | bytes 15840000 | tf_op jit(solution)/shard_map/apply/pallas_call | solution.py:26
  90.4 2.5 %apply.13.refs_14_ = f32[32,1664]{1,0:T(8,128)S(1)} custom-call(f32[32,1536]{1,0:T(8,128)S(1)} %collective-permute-done.17.refs_0_.refs_2_, bf16[160,1536]{1,0:T(8,128)(2,1)S(1)} %collective-permute-done.3.refs_0_.refs_1_, bf16[1536,512]{1,0:T(8,128)(2,1)S(1)} %get-tuple-element.75.refs_2_.refs_4_, bf16[1536,512]{1,0:T(8,128)(2,1)S(1)} %get-tuple-element.76.refs_3_.refs_5_, ...), custom_call_target="tpu_custom_call" | custom-call | bytes 7920000 | tf_op jit(solution)/shard_map/apply/pallas_call | solution.py:26
  106.0 3.3 %collective-permute-done.24 = f32[32,384]{1,0:T(8,128)S(1)} collective-permute-done((f32[32,384]{1,0:T(8,128)S(1)}, f32[32,384]{1,0:T(8,128)S(1)}, u32[]{:S(2)}, u32[]{:S(2)}) %collective-permute-start.24) | collective-permute-done | bytes 49184 | tf_op jit(solution)/shard_map/ppermute | solution.py:43
  114.0 5.5 %apply.15.refs_12_ = f32[32,3200]{1,0:T(8,128)S(1)} custom-call(f32[32,1536]{1,0:T(8,128)S(1)} %constant_dynamic-update-slice_fusion.6.refs_0_, bf16[160,1536]{1,0:T(8,128)(2,1)S(1)} %pad_maximum_fusion.refs_0_.refs_1_, f32[32,1536]{1,0:T(8,128)S(1)} %constant_dynamic-update-slice_fusion.2.refs_0_.refs_2_, ...), custom_call_target="tpu_custom_call" | custom-call | bytes 15840000 | tf_op jit(solution)/shard_map/apply/pallas_call | solution.py:26
  119.5 4.8 %apply.16.refs_12_ = f32[32,3200]{1,0:T(8,128)S(1)} custom-call(f32[32,1536]{1,0:T(8,128)S(1)} %collective-permute-done.29.refs_0_, bf16[160,1536]{1,0:T(8,128)(2,1)S(1)} %collective-permute-done.9.refs_0_.refs_1_, f32[32,1536]{1,0:T(8,128)S(1)} %copy-done.5, f32[32,128]{1,0:T(8,128)S(1)} %get-tuple-element.116.refs_3_.coef_ref, ...), custom_call_target="tpu_custom_call" | custom-call | bytes 15840000 | tf_op jit(solution)/shard_map/apply/pallas_call | solution.py:26
  124.3 4.8 %apply.17.refs_15_ = f32[32,3200]{1,0:T(8,128)S(1)} custom-call(f32[32,1536]{1,0:T(8,128)S(1)} %collective-permute-done.28.refs_0_, bf16[160,1536]{1,0:T(8,128)(2,1)S(1)} %collective-permute-done.8.refs_0_.refs_1_, f32[32,1536]{1,0:T(8,128)S(1)} %collective-permute-done.18.refs_0_.refs_2_, f32[32,128]{1,0:T(8,128)S(1)} %get-tuple-element.116.refs_3_.coef_ref, ...), custom_call_target="tpu_custom_call" | custom-call | bytes 15840000 | tf_op jit(solution)/shard_map/apply/pallas_call | solution.py:26
  129.2 3.3 %apply.18.refs_16_ = f32[32,1664]{1,0:T(8,128)S(1)} custom-call(f32[32,1536]{1,0:T(8,128)S(1)} %collective-permute-done.27.refs_0_, bf16[160,1536]{1,0:T(8,128)(2,1)S(1)} %collective-permute-done.3.refs_0_.refs_1_, f32[32,1536]{1,0:T(8,128)S(1)} %collective-permute-done.17.refs_0_.refs_2_, f32[32,128]{1,0:T(8,128)S(1)} %get-tuple-element.116.refs_3_.coef_ref, ...), custom_call_target="tpu_custom_call" | custom-call | bytes 7920000 | tf_op jit(solution)/shard_map/apply/pallas_call | solution.py:26
  137.9 2.5 %collective-permute-done.31.m1 = f32[32,512]{1,0:T(8,128)S(1)} collective-permute-done((f32[32,512]{1,0:T(8,128)S(1)}, f32[32,512]{1,0:T(8,128)S(1)}, u32[]{:S(2)}, u32[]{:S(2)}) %collective-permute-start.31) | collective-permute-done | bytes 65568 | tf_op jit(solution)/shard_map/ppermute | solution.py:43
  143.3 18.0 %all_to_all.5.sums_ref = f32[64,8,128]{2,1,0:T(8,128)S(1)} all-to-all(f32[64,8,128]{2,1,0:T(8,128)S(1)} %broadcast_in_dim.2), channel_id=1, replica_groups=mesh['x'=4,'y'=4,'zl'=2,'c'=2,'zh'=2] {'x','y','zl','zh'}, dimensions={0} | all-to-all | bytes 524288 | tf_op jit(solution)/shard_map/all_to_all | solution.py:449
  (110 shorter events, 43.5 us)
Async XLA Ops:
  1.6 8.6 %collective-permute-start.2 = (bf16[160,384]{1,0:T(8,128)(2,1)S(1)}, bf16[160,384]{1,0:T(8,128)(2,1)S(1)}, u32[]{:S(2)}, u32[]{:S(2)}) collective-permute-start(bf16[160,384]{1,0:T(8,128)(2,1)S(1)} %pack.1), channel_id=1, source_target_pairs={{0,16},{8,24},{16,0},{24,8},{1,17},{9,25},{17,1},{25,9},{2,18},{10... | collective-permute-start | bytes 368648 | tf_op jit(solution)/shard_map/ppermute | solution.py:43
  4.9 7.9 %collective-permute-start.1 = (bf16[160,384]{1,0:T(8,128)(2,1)S(1)}, bf16[160,384]{1,0:T(8,128)(2,1)S(1)}, u32[]{:S(2)}, u32[]{:S(2)}) collective-permute-start(bf16[160,384]{1,0:T(8,128)(2,1)S(1)} %pack.1), channel_id=1, source_target_pairs={{0,24},{8,16},{16,8},{24,0},{1,25},{9,17},{17,9},{25,1},{2,26},{10... | collective-permute-start | bytes 368648 | tf_op jit(solution)/shard_map/ppermute | solution.py:43
  6.0 6.9 %collective-permute-start = (bf16[160,384]{1,0:T(8,128)(2,1)S(1)}, bf16[160,384]{1,0:T(8,128)(2,1)S(1)}, u32[]{:S(2)}, u32[]{:S(2)}) collective-permute-start(bf16[160,384]{1,0:T(8,128)(2,1)S(1)} %pack.1), channel_id=1, source_target_pairs={{0,8},{8,0},{16,24},{24,16},{1,9},{9,1},{17,25},{25,17},{2,10},{10... | collective-permute-start | bytes 368648 | tf_op jit(solution)/shard_map/ppermute | solution.py:43
  6.0 13.9 %collective-permute-start.7 = (bf16[64,768]{1,0:T(8,128)(2,1)S(1)}, bf16[64,768]{1,0:T(8,128)(2,1)S(1)}, u32[]{:S(2)}, u32[]{:S(2)}) collective-permute-start(bf16[64,768]{1,0:T(8,128)(2,1)S(1)} %pad_maximum_fusion.2), channel_id=1, source_target_pairs={{0,5},{1,4},{4,1},{5,0},{2,7},{3,6},{6,3},{7,2},{8,13},{9,12},{12,... | collective-permute-start | bytes 294920 | tf_op jit(solution)/shard_map/ppermute | solution.py:43
  10.2 9.8 %collective-permute-start.6 = (bf16[64,768]{1,0:T(8,128)(2,1)S(1)}, bf16[64,768]{1,0:T(8,128)(2,1)S(1)}, u32[]{:S(2)}, u32[]{:S(2)}) collective-permute-start(bf16[64,768]{1,0:T(8,128)(2,1)S(1)} %pad_maximum_fusion.2), channel_id=1, source_target_pairs={{0,4},{1,5},{4,0},{5,1},{2,6},{3,7},{6,2},{7,3},{8,12},{9,13},{12,... | collective-permute-start | bytes 294920 | tf_op jit(solution)/shard_map/ppermute | solution.py:43
  10.2 6.4 %collective-permute-start.5 = (bf16[64,768]{1,0:T(8,128)(2,1)S(1)}, bf16[64,768]{1,0:T(8,128)(2,1)S(1)}, u32[]{:S(2)}, u32[]{:S(2)}) collective-permute-start(bf16[64,768]{1,0:T(8,128)(2,1)S(1)} %pad_maximum_fusion.2), channel_id=1, source_target_pairs={{0,1},{1,0},{4,5},{5,4},{2,3},{3,2},{6,7},{7,6},{8,9},{9,8},{12,13... | collective-permute-start | bytes 294920 | tf_op jit(solution)/shard_map/ppermute | solution.py:43
  12.9 14.8 %collective-permute-start.9 = (bf16[160,1536]{1,0:T(8,128)(2,1)S(1)}, bf16[160,1536]{1,0:T(8,128)(2,1)S(1)}, u32[]{:S(2)}, u32[]{:S(2)}) collective-permute-start(bf16[160,1536]{1,0:T(8,128)(2,1)S(1)} %pad_maximum_fusion.refs_0_.refs_1_), channel_id=1, source_target_pairs={{0,32},{32,0},{64,96},{96,64},{1,33},{33,1},{65,97},{97,65},{2,34}... | collective-permute-start | bytes 1474568 | tf_op jit(solution)/shard_map/ppermute | solution.py:43
  14.5 24.0 %collective-permute-start.8 = (bf16[160,1536]{1,0:T(8,128)(2,1)S(1)}, bf16[160,1536]{1,0:T(8,128)(2,1)S(1)}, u32[]{:S(2)}, u32[]{:S(2)}) collective-permute-start(bf16[160,1536]{1,0:T(8,128)(2,1)S(1)} %pad_maximum_fusion.refs_0_.refs_1_), channel_id=1, source_target_pairs={{0,96},{32,64},{64,32},{96,0},{1,97},{33,65},{65,33},{97,1},{2,98}... | collective-permute-start | bytes 1474568 | tf_op jit(solution)/shard_map/ppermute | solution.py:43
  16.6 29.4 %collective-permute-start.3 = (bf16[160,1536]{1,0:T(8,128)(2,1)S(1)}, bf16[160,1536]{1,0:T(8,128)(2,1)S(1)}, u32[]{:S(2)}, u32[]{:S(2)}) collective-permute-start(bf16[160,1536]{1,0:T(8,128)(2,1)S(1)} %pad_maximum_fusion.refs_0_.refs_1_), channel_id=1, source_target_pairs={{0,64},{32,96},{64,0},{96,32},{1,65},{33,97},{65,1},{97,33},{2,66}... | collective-permute-start | bytes 1474568 | tf_op jit(solution)/shard_map/ppermute | solution.py:43
  55.2 5.8 %collective-permute-start.11 = (f32[32,512]{1,0:T(8,128)S(1)}, f32[32,512]{1,0:T(8,128)S(1)}, u32[]{:S(2)}, u32[]{:S(2)}) collective-permute-start(f32[32,512]{1,0:T(8,128)S(1)} %get-tuple-element.71), channel_id=1, source_target_pairs={{0,1},{1,0},{4,5},{5,4},{2,3},{3,2},{6,7},{7,6},{8,9},{9,8},{12,13... | collective-permute-start | bytes 196616 | tf_op jit(solution)/shard_map/ppermute | solution.py:43
  58.5 5.5 %collective-permute-start.12 = (f32[32,512]{1,0:T(8,128)S(1)}, f32[32,512]{1,0:T(8,128)S(1)}, u32[]{:S(2)}, u32[]{:S(2)}) collective-permute-start(f32[32,512]{1,0:T(8,128)S(1)} %get-tuple-element.72), channel_id=1, source_target_pairs={{0,5},{1,4},{4,1},{5,0},{2,7},{3,6},{6,3},{7,2},{8,13},{9,12},{12,... | collective-permute-start | bytes 196616 | tf_op jit(solution)/shard_map/ppermute | solution.py:43
  64.0 8.4 %collective-permute-start.16 = (f32[32,384]{1,0:T(8,128)S(1)}, f32[32,384]{1,0:T(8,128)S(1)}, u32[]{:S(2)}, u32[]{:S(2)}) collective-permute-start(f32[32,384]{1,0:T(8,128)S(1)} %get-tuple-element.74.u0_ref), channel_id=1, source_target_pairs={{0,16},{8,24},{16,0},{24,8},{1,17},{9,25},{17,1},{25,9},{2,18},{10... | collective-permute-start | bytes 147464 | tf_op jit(solution)/shard_map/ppermute | solution.py:43
  66.5 5.9 %collective-permute-start.15 = (f32[32,384]{1,0:T(8,128)S(1)}, f32[32,384]{1,0:T(8,128)S(1)}, u32[]{:S(2)}, u32[]{:S(2)}) collective-permute-start(f32[32,384]{1,0:T(8,128)S(1)} %get-tuple-element.74.u0_ref), channel_id=1, source_target_pairs={{0,24},{8,16},{16,8},{24,0},{1,25},{9,17},{17,9},{25,1},{2,26},{10... | collective-permute-start | bytes 147464 | tf_op jit(solution)/shard_map/ppermute | solution.py:43
  72.5 8.7 %collective-permute-start.19 = (f32[32,1536]{1,0:T(8,128)S(1)}, f32[32,1536]{1,0:T(8,128)S(1)}, u32[]{:S(2)}, u32[]{:S(2)}) collective-permute-start(f32[32,1536]{1,0:T(8,128)S(1)} %constant_dynamic-update-slice_fusion.2.refs_0_.refs_2_), channel_id=1, source_target_pairs={{0,32},{32,0},{64,96},{96,64},{1,33},{33,1},{65,97},{97,65},{2,34}... | collective-permute-start | bytes 589832 | tf_op jit(solution)/shard_map/ppermute | solution.py:43
  72.8 13.1 %collective-permute-start.18 = (f32[32,1536]{1,0:T(8,128)S(1)}, f32[32,1536]{1,0:T(8,128)S(1)}, u32[]{:S(2)}, u32[]{:S(2)}) collective-permute-start(f32[32,1536]{1,0:T(8,128)S(1)} %constant_dynamic-update-slice_fusion.2.refs_0_.refs_2_), channel_id=1, source_target_pairs={{0,96},{32,64},{64,32},{96,0},{1,97},{33,65},{65,33},{97,1},{2,98}... | collective-permute-start | bytes 589832 | tf_op jit(solution)/shard_map/ppermute | solution.py:43
  74.9 15.5 %collective-permute-start.17 = (f32[32,1536]{1,0:T(8,128)S(1)}, f32[32,1536]{1,0:T(8,128)S(1)}, u32[]{:S(2)}, u32[]{:S(2)}) collective-permute-start(f32[32,1536]{1,0:T(8,128)S(1)} %constant_dynamic-update-slice_fusion.2.refs_0_.refs_2_), channel_id=1, source_target_pairs={{0,64},{32,96},{64,0},{96,32},{1,65},{33,97},{65,1},{97,33},{2,66}... | collective-permute-start | bytes 589832 | tf_op jit(solution)/shard_map/ppermute | solution.py:43
  94.8 6.1 %collective-permute-start.21 = (f32[32,512]{1,0:T(8,128)S(1)}, f32[32,512]{1,0:T(8,128)S(1)}, u32[]{:S(2)}, u32[]{:S(2)}) collective-permute-start(f32[32,512]{1,0:T(8,128)S(1)} %get-tuple-element.111), channel_id=1, source_target_pairs={{0,1},{1,0},{4,5},{5,4},{2,3},{3,2},{6,7},{7,6},{8,9},{9,8},{12,13... | collective-permute-start | bytes 196616 | tf_op jit(solution)/shard_map/ppermute | solution.py:43
  96.7 5.5 %collective-permute-start.22 = (f32[32,512]{1,0:T(8,128)S(1)}, f32[32,512]{1,0:T(8,128)S(1)}, u32[]{:S(2)}, u32[]{:S(2)}) collective-permute-start(f32[32,512]{1,0:T(8,128)S(1)} %get-tuple-element.112), channel_id=1, source_target_pairs={{0,5},{1,4},{4,1},{5,0},{2,7},{3,6},{6,3},{7,2},{8,13},{9,12},{12,... | collective-permute-start | bytes 196616 | tf_op jit(solution)/shard_map/ppermute | solution.py:43
  102.4 7.1 %collective-permute-start.26 = (f32[32,384]{1,0:T(8,128)S(1)}, f32[32,384]{1,0:T(8,128)S(1)}, u32[]{:S(2)}, u32[]{:S(2)}) collective-permute-start(f32[32,384]{1,0:T(8,128)S(1)} %get-tuple-element.115.u1_ref), channel_id=1, source_target_pairs={{0,16},{8,24},{16,0},{24,8},{1,17},{9,25},{17,1},{25,9},{2,18},{10... | collective-permute-start | bytes 147464 | tf_op jit(solution)/shard_map/ppermute | solution.py:43
  109.5 9.9 %collective-permute-start.29 = (f32[32,1536]{1,0:T(8,128)S(1)}, f32[32,1536]{1,0:T(8,128)S(1)}, u32[]{:S(2)}, u32[]{:S(2)}) collective-permute-start(f32[32,1536]{1,0:T(8,128)S(1)} %constant_dynamic-update-slice_fusion.6.refs_0_), channel_id=1, source_target_pairs={{0,32},{32,0},{64,96},{96,64},{1,33},{33,1},{65,97},{97,65},{2,34}... | collective-permute-start | bytes 589832 | tf_op jit(solution)/shard_map/ppermute | solution.py:43
  109.7 14.6 %collective-permute-start.28 = (f32[32,1536]{1,0:T(8,128)S(1)}, f32[32,1536]{1,0:T(8,128)S(1)}, u32[]{:S(2)}, u32[]{:S(2)}) collective-permute-start(f32[32,1536]{1,0:T(8,128)S(1)} %constant_dynamic-update-slice_fusion.6.refs_0_), channel_id=1, source_target_pairs={{0,96},{32,64},{64,32},{96,0},{1,97},{33,65},{65,33},{97,1},{2,98}... | collective-permute-start | bytes 589832 | tf_op jit(solution)/shard_map/ppermute | solution.py:43
  111.8 17.4 %collective-permute-start.27 = (f32[32,1536]{1,0:T(8,128)S(1)}, f32[32,1536]{1,0:T(8,128)S(1)}, u32[]{:S(2)}, u32[]{:S(2)}) collective-permute-start(f32[32,1536]{1,0:T(8,128)S(1)} %constant_dynamic-update-slice_fusion.6.refs_0_), channel_id=1, source_target_pairs={{0,64},{32,96},{64,0},{96,32},{1,65},{33,97},{65,1},{97,33},{2,66}... | collective-permute-start | bytes 589832 | tf_op jit(solution)/shard_map/ppermute | solution.py:43
  134.3 6.1 %collective-permute-start.31 = (f32[32,512]{1,0:T(8,128)S(1)}, f32[32,512]{1,0:T(8,128)S(1)}, u32[]{:S(2)}, u32[]{:S(2)}) collective-permute-start(f32[32,512]{1,0:T(8,128)S(1)} %get-tuple-element.118), channel_id=1, source_target_pairs={{0,1},{1,0},{4,5},{5,4},{2,3},{3,2},{6,7},{7,6},{8,9},{9,8},{12,13... | collective-permute-start | bytes 196616 | tf_op jit(solution)/shard_map/ppermute | solution.py:43
  136.2 5.6 %collective-permute-start.32 = (f32[32,512]{1,0:T(8,128)S(1)}, f32[32,512]{1,0:T(8,128)S(1)}, u32[]{:S(2)}, u32[]{:S(2)}) collective-permute-start(f32[32,512]{1,0:T(8,128)S(1)} %get-tuple-element.119), channel_id=1, source_target_pairs={{0,5},{1,4},{4,1},{5,0},{2,7},{3,6},{6,3},{7,2},{8,13},{9,12},{12,... | collective-permute-start | bytes 196616 | tf_op jit(solution)/shard_map/ppermute | solution.py:43
  (19 other events, 234.1 us)
